TPU v7x, 256 devices: a whole 4x4x8 slice. The times are simulated.
256 devices in a mesh: grp: 32 (over x, z), head: 8 (over y, core).
Axes of the slice: x: 4, y: 4, z: 8, core: 2. Of those that a mesh axis runs over, the one named last changes fastest.
Arguments:
- grid_in: bfloat16 [112, 65536], P(None, ('grp', 'head')), may hold values from -6 to 6
- mesh_embed: bfloat16 [32768, 1024], P(('grp', 'head')), may hold values from -6 to 6
- enc_src: int32 [16, 32768], P(None, ('grp', 'head')), may hold values from 0 to 255
- enc_len: int32 [32768], P(('grp', 'head')), may hold values from 1 to 16
- enc_kv_weight: bfloat16 [112, 2048], replicated, may hold values from -0.5 to 0.5
- proc_gain: float32 [1024], replicated, may hold values from 0.1 to 1.9
- qkv_weight: bfloat16 [1024, 3, 1024], P(None, None, 'head'), may hold values from -0.1875 to 0.1875
- out_weight: bfloat16 [1024, 1024], P('head'), may hold values from -0.1875 to 0.1875
- dec_gain: float32 [1024], replicated, may hold values from 0.1 to 1.9
- unpack_pair_projector: bfloat16 [1024, 2048], replicated, may hold values from -0.1875 to 0.1875
- readout_asking_coefficients: bfloat16 [112, 1024], replicated, may hold values from -0.5 to 0.5
- readout_final_coefficients: bfloat16 [100, 1024], replicated, may hold values from -0.1875 to 0.1875
- dec_send: int32 [8192, 32], P(('grp', 'head')), may hold values from 0 to 127
- dec_src: int32 [3, 65536], P(None, ('grp', 'head')), may hold values from 0 to 1023
- dforecast: bfloat16 [100, 65536], P(None, ('grp', 'head')), may hold values from -6 to 6
Outputs:
- estimated_atmosphere: float32 [100, 65536], P(None, ('grp', 'head'))
- vertex_derivative: float32 [32768, 1024], P(('grp', 'head'))
Inputs may be any that keep to these rules, and one draw needn't show every extreme that they name: `enc_src`: each encoder edge of a mesh node names a grid point of the same block. Edges e < enc_len[m] of node m are live. `dec_send`: row (g * 8 + h) * 32 + t lists, slot by slot, the local mesh rows that block g * 8 + h sends to grid block t * 8 + h. `dec_src`: slot r = g * 32 + s of a grid block t * 8 + h is slot s of what block g * 8 + h sends to it.
All inputs are finite; a program needn't handle non-finite values.
Results may differ from a plain program's by a relative error of at most 0.019.
Values may be sent and summed in bfloat16 or wider, within the bound.
A program may use at most 128 MiB of HBM per device.

v0:
```python
import jax
import jax.numpy as jnp
from jax import lax
from jax.sharding import PartitionSpec as P

NH = 16
HEAD_WIDTH = 64
PROGNOSTIC_FIELDS = 100
WIN = 256


EPS = 1e-05


def with_halo(cells, sides, width):
    for axis, dim in sides:
        count = lax.axis_size(axis)
        ends = count - 1
        head = lax.slice_in_dim(cells, 0, width, axis=dim)
        tail = lax.slice_in_dim(cells, cells.shape[dim] - width, cells.shape[dim], axis=dim)
        cells = jnp.concatenate(
            [
                lax.ppermute(tail, axis, [(i, (i + 1) % count) for i in range(ends)]),
                cells,
                lax.ppermute(head, axis, [((i + 1) % count, i) for i in range(ends)]),
            ],
            axis=dim,
        )
    return cells


def norm_rows(rows, gain):
    row_mean = jnp.mean(rows, axis=-1, keepdims=True)
    centred = rows - row_mean
    spread = jnp.mean(centred * centred, axis=-1, keepdims=True)
    inverse = lax.rsqrt(spread + EPS)
    unit_rows = centred * inverse
    return (unit_rows * gain, unit_rows, inverse)


def norm_back(grad_rows, unit_rows, inverse, gain):
    scaled = grad_rows * gain
    first_mean = jnp.mean(scaled, axis=-1, keepdims=True)
    second_mean = jnp.mean(scaled * unit_rows, axis=-1, keepdims=True)
    return inverse * (scaled - first_mean - unit_rows * second_mean)


def encode_block(lattice_fields, embed_rows, sender_vertices, counts, kv_weight):
    entry_extent = embed_rows.shape[1]
    node_count = embed_rows.shape[0]
    fan_in = sender_vertices.shape[0]
    grid_kv = lax.dot_general(
        lattice_fields, kv_weight, (((0,), (0,)), ((), ())), preferred_element_type=jnp.float32
    ).astype(jnp.bfloat16)
    edge_rows = grid_kv[sender_vertices]
    key_portion = edge_rows[..., :entry_extent].reshape(fan_in, node_count, NH, HEAD_WIDTH)
    value_portion = edge_rows[..., entry_extent:].reshape(fan_in, node_count, NH, HEAD_WIDTH)
    query_rows = embed_rows.reshape(node_count, NH, HEAD_WIDTH)
    score_matrix = jnp.einsum(
        "tfl,otfl->otf", query_rows, key_portion, preferred_element_type=jnp.float32
    ) * HEAD_WIDTH ** (-0.5)
    is_live = lax.broadcasted_iota(jnp.int32, (fan_in, node_count), 0) < counts[None, :]
    masked_scores = jnp.where(is_live[..., None], score_matrix, -jnp.inf)
    row_top = jnp.max(masked_scores, axis=0, keepdims=True)
    exp_terms = jnp.exp(masked_scores - row_top)
    softmax_weight = (exp_terms / jnp.sum(exp_terms, axis=0, keepdims=True)).astype(jnp.bfloat16)
    blended_rows = jnp.einsum(
        "xcu,xcut->cut", softmax_weight, value_portion, preferred_element_type=jnp.float32
    )
    return embed_rows.astype(jnp.float32) + blended_rows.reshape(node_count, entry_extent)


def window_attention(query_rows, extended, group_index, group_count):
    total_rows = query_rows.shape[0]
    head_cols = query_rows.shape[1]
    heads_here = head_cols // HEAD_WIDTH
    block_rows = min(512, total_rows)
    base_row = group_index * total_rows
    seq_limit = group_count * total_rows

    def attend_block(start_row):
        query_block = lax.dynamic_slice_in_dim(query_rows, start_row, block_rows, 0).reshape(
            block_rows, heads_here, HEAD_WIDTH
        )
        pair_block = lax.dynamic_slice_in_dim(extended, start_row, block_rows + 2 * WIN, 0)
        key_block = pair_block[:, 0].reshape(block_rows + 2 * WIN, heads_here, HEAD_WIDTH)
        value_block = pair_block[:, 1].reshape(block_rows + 2 * WIN, heads_here, HEAD_WIDTH)
        score_matrix = jnp.einsum(
            "qhd,khd->hqk", query_block, key_block, preferred_element_type=jnp.float32
        ) * HEAD_WIDTH ** (-0.5)
        query_pos = base_row + start_row + lax.broadcasted_iota(jnp.int32, (block_rows, 1), 0)
        key_pos = (
            base_row
            + start_row
            - WIN
            + lax.broadcasted_iota(jnp.int32, (1, block_rows + 2 * WIN), 1)
        )
        pos_gap = query_pos - key_pos
        is_live = (pos_gap <= WIN) & (pos_gap >= -WIN) & (key_pos >= 0) & (key_pos < seq_limit)
        masked_scores = jnp.where(is_live[None], score_matrix, -jnp.inf)
        row_top = jnp.max(masked_scores, axis=-1, keepdims=True)
        exp_terms = jnp.exp(masked_scores - row_top)
        softmax_weight = (exp_terms / jnp.sum(exp_terms, axis=-1, keepdims=True)).astype(
            jnp.bfloat16
        )
        blended_rows = jnp.einsum(
            "hqk,khd->qhd", softmax_weight, value_block, preferred_element_type=jnp.float32
        )
        return blended_rows.reshape(block_rows, head_cols).astype(jnp.bfloat16)

    starts = jnp.arange(total_rows // block_rows, dtype=jnp.int32) * block_rows
    return lax.map(attend_block, starts).reshape(total_rows, head_cols)


def readout_tile(
    lattice_fields,
    neighbour_pairing,
    sender_vertices,
    q_weight,
    readout_result,
    upstream_derivative,
):
    point_count = lattice_fields.shape[1]
    entry_extent = q_weight.shape[1]
    fan_in = sender_vertices.shape[0]
    score_scale = HEAD_WIDTH ** (-0.5)
    query_rows = lax.dot_general(
        lattice_fields, q_weight, (((0,), (0,)), ((), ())), preferred_element_type=jnp.float32
    ).astype(jnp.bfloat16)
    query_heads = query_rows.reshape(point_count, NH, HEAD_WIDTH)
    edge_rows = neighbour_pairing[sender_vertices]
    key_portion = edge_rows[..., :entry_extent].reshape(fan_in, point_count, NH, HEAD_WIDTH)
    value_portion = edge_rows[..., entry_extent:].reshape(fan_in, point_count, NH, HEAD_WIDTH)
    score_matrix = (
        jnp.einsum("pnd,epnd->epn", query_heads, key_portion, preferred_element_type=jnp.float32)
        * score_scale
    )
    row_top = jnp.max(score_matrix, axis=0, keepdims=True)
    exp_terms = jnp.exp(score_matrix - row_top)
    softmax_weight = exp_terms / jnp.sum(exp_terms, axis=0, keepdims=True)
    rounded = softmax_weight.astype(jnp.bfloat16)
    blended_rows = jnp.einsum(
        "epn,epnd->pnd", rounded, value_portion, preferred_element_type=jnp.float32
    )
    result_lines = blended_rows.reshape(point_count, entry_extent).astype(jnp.bfloat16)
    estimated_atmosphere = lattice_fields[:PROGNOSTIC_FIELDS].astype(jnp.float32) + lax.dot_general(
        readout_result, result_lines, (((1,), (1,)), ((), ())), preferred_element_type=jnp.float32
    )
    back_grad = lax.dot_general(
        upstream_derivative,
        readout_result,
        (((0,), (0,)), ((), ())),
        preferred_element_type=jnp.float32,
    ).reshape(point_count, NH, HEAD_WIDTH)
    along_value = jnp.einsum("pnd,epnd->epn", back_grad, value_portion.astype(jnp.float32))
    score_grad = softmax_weight * (
        along_value - jnp.sum(softmax_weight * along_value, axis=0, keepdims=True)
    )
    key_grad = score_grad[..., None] * query_heads.astype(jnp.float32) * score_scale
    value_grad = rounded.astype(jnp.float32)[..., None] * back_grad
    edge_grad = jnp.concatenate(
        [
            key_grad.reshape(fan_in, point_count, entry_extent),
            value_grad.reshape(fan_in, point_count, entry_extent),
        ],
        axis=-1,
    )
    adjacent_sensitivity = jax.ops.segment_sum(
        edge_grad.reshape(fan_in * point_count, 2 * entry_extent),
        sender_vertices.reshape(fan_in * point_count),
        num_segments=neighbour_pairing.shape[0],
    )
    return (estimated_atmosphere, adjacent_sensitivity)


def send_rows(payload):
    return lax.all_to_all(payload, "grp", split_axis=0, concat_axis=0, tiled=True)


def body(
    grid_in,
    mesh_embed,
    enc_src,
    enc_len,
    enc_kv_weight,
    proc_gain,
    qkv_weight,
    out_weight,
    dec_gain,
    unpack_pair_projector,
    readout_asking_coefficients,
    readout_final_coefficients,
    dec_send,
    dec_src,
    dforecast,
):
    hidden = encode_block(grid_in, mesh_embed, enc_src, enc_len, enc_kv_weight)
    normed, _, _ = norm_rows(hidden, proc_gain)
    normed_in = normed.astype(jnp.bfloat16)
    local_weight = qkv_weight.reshape(qkv_weight.shape[0], -1)
    triple = jnp.dot(
        lax.all_gather(normed_in, "head", axis=0, tiled=True),
        local_weight,
        preferred_element_type=jnp.float32,
    ).astype(jnp.bfloat16)
    head_cols = triple.shape[1] // 3
    triple = triple.reshape(triple.shape[0], 3, head_cols)
    query_rows = triple[:, 0]
    pair_rows = triple[:, 1:]
    extended = with_halo(pair_rows, (("grp", 0),), WIN)
    attended = window_attention(query_rows, extended, lax.axis_index("grp"), lax.axis_size("grp"))
    own_rows = mesh_embed.shape[0]
    projected = lax.psum_scatter(
        jnp.dot(attended, out_weight, preferred_element_type=jnp.float32).astype(jnp.bfloat16),
        "head",
        scatter_dimension=0,
        tiled=True,
    ).astype(jnp.float32)
    state_rows = hidden + projected
    dec_norm, unit_rows, inverse = norm_rows(state_rows, dec_gain)
    dec_in = dec_norm.astype(jnp.bfloat16)
    partner_number = dec_send.shape[0]
    bucket_capacity = dec_send.shape[1]
    arrived = send_rows(dec_in[dec_send])
    neighbour_pairing = jnp.dot(
        arrived.reshape(partner_number * bucket_capacity, -1),
        unpack_pair_projector,
        preferred_element_type=jnp.float32,
    ).astype(jnp.bfloat16)
    estimated_atmosphere, adjacent_sensitivity = readout_tile(
        grid_in,
        neighbour_pairing,
        dec_src,
        readout_asking_coefficients,
        readout_final_coefficients,
        dforecast,
    )
    slot_rounded = adjacent_sensitivity.astype(jnp.bfloat16)
    element_terms_list = lax.dot_general(
        slot_rounded,
        unpack_pair_projector,
        (((1,), (1,)), ((), ())),
        preferred_element_type=jnp.float32,
    )
    returned = lax.all_to_all(
        element_terms_list.reshape(partner_number, bucket_capacity, -1).astype(jnp.bfloat16),
        "grp",
        split_axis=0,
        concat_axis=0,
        tiled=True,
    ).astype(jnp.float32)
    back_rows = returned.reshape(partner_number * bucket_capacity, -1)
    entry_derivative = jax.ops.segment_sum(back_rows, dec_send.reshape(-1), num_segments=own_rows)
    vertex_derivative = norm_back(entry_derivative, unit_rows, inverse, dec_gain)
    return (estimated_atmosphere, vertex_derivative)


def solution(mesh):
    return jax.shard_map(
        body,
        mesh=mesh,
        in_specs=(
            P(None, ("grp", "head")),
            P(("grp", "head"), None),
            P(None, ("grp", "head")),
            P(("grp", "head")),
            P(),
            P(),
            P(None, None, "head"),
            P("head", None),
            P(),
            P(),
            P(),
            P(),
            P(("grp", "head"), None),
            P(None, ("grp", "head")),
            P(None, ("grp", "head")),
        ),
        out_specs=(P(None, ("grp", "head")), P(("grp", "head"), None)),
        check_vma=False,
    )
```

profile of v0, /device:TPU:24, one launch (start us, length us, event | category | flops | bytes accessed | tf_op | source)
XLA Modules:
  0.0 375.5 jit_solution(5850607213814970563)
XLA Ops:
  9.5 11.0 %gather_fusion = bf16[2048,2048]{1,0:T(8,128)(2,1)} fusion(bf16[256,2048]{1,0:T(8,128)(2,1)S(1)} %convolution_convert_fusion.1, s32[2048]{0:T(1024)S(1)} %fusion.39), kind=kCustom, calls=%fused_computation | custom fusion | bytes 16785408 | tf_op jit(solution)/shard_map/gather | solution.py:55
  20.5 6.1 %fusion.44 = (bf16[16,128,1024]{2,1,0:T(8,128)(2,1)}, bf16[16,128,1024]{2,1,0:T(8,128)(2,1)}) fusion(bf16[16,128,2048]{2,1,0:T(8,128)(2,1)} %bitcast.129), kind=kLoop, calls=%fused_computation.107 | loop fusion | bytes 16777216 | tf_op jit(solution)/shard_map/slice | solution.py:56
  26.5 6.4 %copy.92 = bf16[16,128,1024]{1,2,0:T(8,128)(2,1)} copy(bf16[16,128,1024]{2,1,0:T(8,128)(2,1)} %get-tuple-element.102) | data formatting | bytes 8388608
  33.2 3.8 %multiply_reduce_fusion.1 = f32[128,16,16]{0,1,2:T(8,128)S(1)} fusion(f32[128,16,64]{0,2,1:T(8,128)S(1)} %bitcast_convert_fusion.3, bf16[16,128,1024]{1,2,0:T(8,128)(2,1)} %copy.92), kind=kLoop, calls=%fused_computation.33 | loop fusion | flops 6258688 | bytes 4849664 | tf_op jit(solution)/shard_map/tfl,otfl->otf/dot_general | solution.py:59
  37.2 6.4 %copy.93 = bf16[16,128,1024]{1,2,0:T(8,128)(2,1)} copy(bf16[16,128,1024]{2,1,0:T(8,128)(2,1)} %get-tuple-element.103) | data formatting | bytes 8388608
  43.6 3.4 multiply_reduce_fusion
  48.8 29.2 %all-gather.2.cloned.1.call-done = bf16[1024,1024]{1,0:T(8,128)(2,1)} async-done(((bf16[128,1024]{1,0:T(8,128)(2,1)}), bf16[1024,1024]{1,0:T(8,128)(2,1)}) %all-gather.2.cloned.1.call-update) | async-done | bytes 2097168 | tf_op jit(solution)/shard_map/all_gather | solution.py:202
  78.0 2.6 convolution_convert_fusion.3
  80.7 3.5 collective-permute-start
  87.3 4.1 %collective-permute-done.1 = bf16[256,2,128]{0,2,1:T(8,128)(2,1)S(1)} collective-permute-done((bf16[256,2,128]{0,2,1:T(8,128)(2,1)S(1)}, bf16[256,2,128]{0,2,1:T(8,128)(2,1)S(1)}, u32[]{:S(2)}, u32[]{:S(2)}) %collective-permute-start.1) | collective-permute-done | bytes 131104 | tf_op jit(solution)/shard_map/ppermute | solution.py:25
  91.5 26.7 %while.12 = (s32[]{:T(128)}, bf16[2,512,128]{2,1,0:T(8,128)(2,1)}, s32[2]{0:T(128)S(1)}, bf16[1536,2,128]{0,2,1:T(8,128)(2,1)S(1)}, s32[]{:T(128)}, /*index=5*/b...) while((s32[]{:T(128)}, bf16[2,512,128]{2,1,0:T(8,128)(2,1)}, ...), condition=%wide.region_7.8_spmd, body=%wide.region_4.7_spmd.sunk | while | flops 277943808 | bytes 14180660 | solution.py:112
  97.4 3.5 fusion.80
  100.9 3.1 fusion.81
  110.7 3.5 fusion.80
  114.3 3.1 fusion.81
  118.2 3.0 convolution_convert_fusion.2
  121.3 34.5 %reduce-scatter.2.cloned.1.call-done = bf16[128,1024]{1,0:T(8,128)(2,1)} async-done(((bf16[1024,1024]{1,0:T(8,128)(2,1)}), bf16[128,1024]{1,0:T(8,128)(2,1)}) %reduce-scatter.2.cloned.1.call-update) | async-done | bytes 262160 | tf_op jit(solution)/shard_map/reduce_scatter | solution.py:213
  157.4 5.4 %gather_fusion.1 = bf16[1024,1024]{1,0:T(8,128)(2,1)} fusion(bf16[128,1024]{1,0:T(8,128)(2,1)S(1)} %multiply_convert_fusion, s32[1024]{0:T(1024)S(1)} %broadcast_clamp_fusion), kind=kCustom, calls=%fused_computation.1 | custom fusion | bytes 4198400 | tf_op jit(solution)/shard_map/gather | solution.py:224
  162.8 10.3 %all-to-all-start = ((bf16[32,32,1024]{2,1,0:T(8,128)(2,1)}), bf16[32,32,1024]{2,1,0:T(8,128)(2,1)}, u32[]{:S(2)}, u32[]{:S(2)}) async-start(bf16[32,32,1024]{2,1,0:T(8,128)(2,1)} %bitcast.139), calls=%async_computation.1 | async-start | bytes 4194304 | tf_op jit(solution)/shard_map/all_to_all | solution.py:177
  177.4 3.6 copy.55
  183.0 3.6 copy.54
  187.7 36.4 %all-to-all-done = bf16[32,32,1024]{2,1,0:T(8,128)(2,1)} async-done(((bf16[32,32,1024]{2,1,0:T(8,128)(2,1)}), bf16[32,32,1024]{2,1,0:T(8,128)(2,1)}, u32[]{:S(2)}, u32[]{:S(2)}) %all-to-all-start) | async-done | bytes 2097184 | tf_op jit(solution)/shard_map/all_to_all | solution.py:177
  224.1 9.2 %convolution_convert_fusion = bf16[1024,2048]{1,0:T(8,128)(2,1)} fusion(bf16[1024,1024]{1,0:T(8,128)(2,1)} %bitcast.27, bf16[1024,2048]{1,0:T(8,128)(2,1)} %param.26), kind=kOutput, calls=%fused_computation.41 | convolution fusion | flops 4297064448 | bytes 10485760 | tf_op jit(solution)/shard_map/dot_general | solution.py:225
  233.3 9.9 %gather_fusion.2 = bf16[768,2048]{1,0:T(8,128)(2,1)} fusion(bf16[1024,2048]{1,0:T(8,128)(2,1)} %convolution_convert_fusion, s32[1024]{0:T(1024)S(1)} %pad_clamp_fusion), kind=kCustom, calls=%fused_computation.2 | custom fusion | bytes 6294528 | tf_op jit(solution)/shard_map/gather | solution.py:131
  243.2 3.5 fusion.45
  260.6 3.1 pad_maximum_fusion
  263.7 6.6 %copy.56 = f32[768,2048]{1,0:T(8,128)} copy(f32[768,2048]{0,1:T(8,128)} %pad_maximum_fusion) | data formatting | bytes 12582912 | tf_op jit(solution)/shard_map/concatenate | solution.py:161
  270.3 18.6 %scatter_custom_fusion = f32[1024,2048]{1,0:T(8,128)} fusion(s32[768]{0:T(1024)S(1)} %reshape.271, f32[768,2048]{1,0:T(8,128)} %copy.56, f32[]{:T(128)} %constant.94.clone.1), kind=kCustom, calls=%fused_computation.39 | custom fusion | flops 1572864 | bytes 8389120 | tf_op jit(solution)/shard_map/scatter-add | solution.py:168
  288.9 10.5 %fusion.23 = bf16[1024,1024]{1,0:T(8,128)(2,1)} fusion(bf16[1024,2048]{1,0:T(8,128)(2,1)} %param.26, f32[1024,2048]{1,0:T(8,128)} %scatter_custom_fusion), kind=kOutput, calls=%fused_computation.47 | convolution fusion | flops 4298113024 | bytes 14680064 | tf_op jit(solution)/shard_map/dot_general | solution.py:239
  299.4 7.7 %all-to-all-start.1 = ((bf16[32,32,1024]{2,1,0:T(8,128)(2,1)}), bf16[32,32,1024]{2,1,0:T(8,128)(2,1)}, u32[]{:S(2)}, u32[]{:S(2)}) async-start(bf16[32,32,1024]{2,1,0:T(8,128)(2,1)} %bitcast.146), calls=%async_computation.2 | async-start | bytes 4194304 | tf_op jit(solution)/shard_map/all_to_all | solution.py:245
  308.4 48.9 %all-to-all-done.1 = bf16[32,32,1024]{2,1,0:T(8,128)(2,1)} async-done(((bf16[32,32,1024]{2,1,0:T(8,128)(2,1)}), bf16[32,32,1024]{2,1,0:T(8,128)(2,1)}, u32[]{:S(2)}, u32[]{:S(2)}) %all-to-all-start.1) | async-done | bytes 2097184 | tf_op jit(solution)/shard_map/all_to_all | solution.py:245
  357.4 9.8 %scatter_custom_fusion.1 = f32[128,1024]{1,0:T(8,128)S(1)} fusion(s32[1024]{0:T(1024)S(1)} %reshape.279, bf16[1024,1024]{1,0:T(8,128)(2,1)} %bitcast.45, f32[]{:T(128)} %constant.94.clone.1), kind=kCustom, calls=%fused_computation.35 | custom fusion | flops 2097152 | bytes 2621444 | tf_op jit(solution)/shard_map/scatter-add | solution.py:253
  (124 shorter events, 38.1 us)
Async XLA Ops:
  7.2 1.0 copy-start
  7.2 70.8 %all-gather.2.cloned.1.call-start = ((), (), s32[]{:S(2)}) async-start(), calls=%async_computation.3 | async-start | bytes 2359296 | tf_op jit(solution)/shard_map/all_gather | solution.py:202
  26.5 6.4 %copy-start.4 = (bf16[128,1024]{1,0:T(8,128)(2,1)S(1)}, bf16[128,1024]{1,0:T(8,128)(2,1)}, u32[]{:S(2)}) copy-start(bf16[128,1024]{1,0:T(8,128)(2,1)} %param.18) | copy-start | bytes 786436
  26.5 6.7 %copy-start.17 = (s32[128]{0:T(128)S(1)}, s32[128]{0:T(128)}, u32[]{:S(2)}) copy-start(s32[128]{0:T(128)} %param.20) | copy-start | bytes 1540
  43.6 4.0 %copy-start.16 = (f32[1024]{0:T(1024)S(1)}, f32[1024]{0:T(1024)}, u32[]{:S(2)}) copy-start(f32[1024]{0:T(1024)} %param.22) | copy-start | bytes 12292
  43.6 4.9 %copy-start.6 = (bf16[1024,3,128]{2,0,1:T(8,128)(2,1)S(1)}, bf16[1024,3,128]{2,0,1:T(8,128)(2,1)}, u32[]{:S(2)}) copy-start(bf16[1024,3,128]{2,0,1:T(8,128)(2,1)} %param.23) | copy-start | bytes 2359300
  48.4 107.5 %reduce-scatter.2.cloned.1.call-start = ((), (), s32[]{:S(2)}) async-start(), calls=%async_computation.4 | async-start | bytes 2359296 | tf_op jit(solution)/shard_map/reduce_scatter | solution.py:213
  80.7 6.6 %collective-permute-start = (bf16[256,2,128]{0,2,1:T(8,128)(2,1)S(1)}, bf16[256,2,128]{0,2,1:T(8,128)(2,1)S(1)}, u32[]{:S(2)}, u32[]{:S(2)}) collective-permute-start(bf16[256,2,128]{0,2,1:T(8,128)(2,1)S(1)} %get-tuple-element.106), channel_id=1, source_target_pairs={{0,8},{8,16},{16,24},{24,32},{32,40},{40,48},{48,56},{56,64},{64,7... | collective-permute-start | bytes 393224 | tf_op jit(solution)/shard_map/ppermute | solution.py:23
  84.2 7.3 %collective-permute-start.1 = (bf16[256,2,128]{0,2,1:T(8,128)(2,1)S(1)}, bf16[256,2,128]{0,2,1:T(8,128)(2,1)S(1)}, u32[]{:S(2)}, u32[]{:S(2)}) collective-permute-start(bf16[256,2,128]{0,2,1:T(8,128)(2,1)S(1)} %get-tuple-element.107), channel_id=1, source_target_pairs={{8,0},{16,8},{24,16},{32,24},{40,32},{48,40},{56,48},{64,56},{72,6... | collective-permute-start | bytes 393224 | tf_op jit(solution)/shard_map/ppermute | solution.py:25
  91.5 26.7 %copy-start.8 = (bf16[128,1024]{1,0:T(8,128)(2,1)S(1)}, bf16[128,1024]{1,0:T(8,128)(2,1)}, u32[]{:S(2)}) copy-start(bf16[128,1024]{1,0:T(8,128)(2,1)} %param.24) | copy-start | bytes 786436
  100.9 3.2 copy-start.9
  104.1 0.7 copy-start.10
  114.2 3.2 copy-start.9
  117.5 0.7 copy-start.10
  118.2 3.1 copy-start.12
  118.2 39.0 %copy-start.14 = (f32[1024]{0:T(1024)S(1)}, f32[1024]{0:T(1024)}, u32[]{:S(2)}) copy-start(f32[1024]{0:T(1024)} %param.25) | copy-start | bytes 12292
  162.7 10.3 %copy-start.15 = (s32[3,256]{1,0:T(4,128)S(1)}, s32[3,256]{1,0:T(4,128)}, u32[]{:S(2)}) copy-start(s32[3,256]{1,0:T(4,128)} %param.30) | copy-start | bytes 9220
  162.7 10.4 %copy-start.7 = (bf16[112,256]{1,0:T(8,128)(2,1)S(1)}, bf16[112,256]{1,0:T(8,128)(2,1)}, u32[]{:S(2)}) copy-start(bf16[112,256]{1,0:T(8,128)(2,1)} %param.17) | copy-start | bytes 172036
  162.7 10.4 %copy-start.11 = (bf16[112,1024]{1,0:T(8,128)(2,1)S(1)}, bf16[112,1024]{1,0:T(8,128)(2,1)}, u32[]{:S(2)}) copy-start(bf16[112,1024]{1,0:T(8,128)(2,1)} %param.27) | copy-start | bytes 688132
  162.7 10.9 %copy-start.5 = (bf16[100,1024]{1,0:T(8,128)(2,1)S(1)}, bf16[100,1024]{1,0:T(8,128)(2,1)}, u32[]{:S(2)}) copy-start(bf16[100,1024]{1,0:T(8,128)(2,1)} %param.28) | copy-start | bytes 614404
  162.8 10.9 %copy-start.13 = (bf16[100,256]{1,0:T(8,128)(2,1)S(1)}, bf16[100,256]{1,0:T(8,128)(2,1)}, u32[]{:S(2)}) copy-start(bf16[100,256]{1,0:T(8,128)(2,1)} %param.31) | copy-start | bytes 153604
  162.8 61.3 %all-to-all-start = ((bf16[32,32,1024]{2,1,0:T(8,128)(2,1)}), bf16[32,32,1024]{2,1,0:T(8,128)(2,1)}, u32[]{:S(2)}, u32[]{:S(2)}) async-start(bf16[32,32,1024]{2,1,0:T(8,128)(2,1)} %bitcast.139), calls=%async_computation.1 | async-start | bytes 4194304 | tf_op jit(solution)/shard_map/all_to_all | solution.py:177
  256.4 1.9 copy-start.2
  258.3 1.9 copy-start.3
  299.4 58.0 %all-to-all-start.1 = ((bf16[32,32,1024]{2,1,0:T(8,128)(2,1)}), bf16[32,32,1024]{2,1,0:T(8,128)(2,1)}, u32[]{:S(2)}, u32[]{:S(2)}) async-start(bf16[32,32,1024]{2,1,0:T(8,128)(2,1)} %bitcast.146), calls=%async_computation.2 | async-start | bytes 4194304 | tf_op jit(solution)/shard_map/all_to_all | solution.py:245
  307.2 61.3 %copy-start.1 = (bf16[112,2048]{1,0:T(8,128)(2,1)S(1)}, bf16[112,2048]{1,0:T(8,128)(2,1)}, u32[]{:S(2)}) copy-start(bf16[112,2048]{1,0:T(8,128)(2,1)} %param.21) | copy-start | bytes 1376260
Sparse Core Ops, SparseCore 0:
  48.5 29.4 all-gather.1
  121.4 34.4 reduce-scatter.1
where the time goes:
time: 382 us; the launch traced here: 376 us
  waiting for transfers between devices  155 us (41%)
  local copies, waits for them, and re-layouts  81.9 us (21%)
  other arithmetic  51.3 us (13%)
  matrix products  41.3 us (11%)
  starting transfers between devices  23 us (6%)
  between operations  14.7 us (4%)
  loops' own time  8.49 us (2%)
    all_to_all x1, waiting for transfers between devices, body(): lax.all_to_all(element_terms_list.reshape(partner_number, bucket_capacity...  48.9 us
    all_to_all x1, waiting for transfers between devices, send_rows(): lax.all_to_all(payload, 'grp', split_axis=0, concat_axis=0, tiled=True)  36.4 us
    reduce_scatter x1, waiting for transfers between devices, body(): lax.psum_scatter(jnp.dot(attended, out_weight, preferred_element_type=jnp...  34.5 us
    all_gather x1, waiting for transfers between devices, body(): lax.all_gather(normed_in, 'head', axis=0, tiled=True)  29.2 us
    unnamed x41, local copies, waits for them, and re-layouts  21.5 us
    scatter-add x1, other arithmetic, readout_tile(): jax.ops.segment_sum(edge_grad.reshape(fan_in * point_count, 2 * entry_ext...  18.6 us
    gather x1, local copies, waits for them, and re-layouts, encode_block(): edge_rows = grid_kv[sender_vertices]  11 us
    dot_general x1, matrix products, body(): lax.dot_general(slot_rounded, unpack_pair_projector, (((1,), (1,)), ((),...  10.5 us
  transfers between devices with their start and end apart: 6, of which 6 were waited for; matrix products, arithmetic and copies ran while one was open for 4% of the time, Pallas kernels for 0%

commit v1 on v0

v1 whole, which is shorter than its diff:
```python
import jax
import jax.numpy as jnp
from jax import lax
from jax.experimental import pallas as pl
from jax.experimental.pallas import tpu as pltpu
from jax.sharding import PartitionSpec as P

F32 = jnp.float32
BF = jnp.bfloat16
EPS = 1e-05
SCALE = 0.125


def nn(a, b):
    return lax.dot_general(a, b, (((1,), (0,)), ((), ())), preferred_element_type=F32)


def nt(a, b):
    return lax.dot_general(a, b, (((1,), (1,)), ((), ())), preferred_element_type=F32)


def tn(a, b):
    return lax.dot_general(a, b, (((0,), (0,)), ((), ())), preferred_element_type=F32)


def half_masks():
    lane = lax.broadcasted_iota(jnp.int32, (1, 128), 1)
    return [(lane < 64).astype(F32).astype(BF), (lane >= 64).astype(F32).astype(BF)]


def norm_rows(rows):
    row_mean = jnp.mean(rows, axis=-1, keepdims=True)
    centred = rows - row_mean
    spread = jnp.mean(centred * centred, axis=-1, keepdims=True)
    inverse = lax.rsqrt(spread + EPS)
    return centred * inverse, inverse


def encode(grid_ref, emb_ref, src_ref, len_ref, wkv_ref, hid_ref):
    points = grid_ref.shape[1]
    nodes = emb_ref.shape[0]
    pid = lax.broadcasted_iota(jnp.int32, (points, nodes), 0)
    count = jnp.zeros((points, nodes), F32)
    lens = len_ref[...]
    for e in range(src_ref.shape[0]):
        row = jnp.where(e < lens, src_ref[e : e + 1, :], -1)
        count += (pid == row).astype(F32)
    dead = jnp.where(count > 0, 0.0, -jnp.inf)
    grid_t = grid_ref[...].T
    masks = half_masks()

    def pair(j, _):
        cols = pl.ds(pl.multiple_of(j * 128, 128), 128)
        vcols = pl.ds(pl.multiple_of(j * 128 + 1024, 128), 128)
        keys = nn(grid_t, wkv_ref[:, cols]).astype(BF)
        values = nn(grid_t, wkv_ref[:, vcols]).astype(BF)
        emb = emb_ref[:, cols]
        weights = []
        for n in range(2):
            score = nt(keys, emb * masks[n]) * SCALE + dead
            top = jnp.max(score, axis=0, keepdims=True)
            term = jnp.exp(score - top) * count
            weights.append((term / jnp.sum(term, axis=0, keepdims=True)).astype(BF))
        mixed = tn(weights[0], values * masks[0]) + tn(weights[1], values * masks[1])
        hid_ref[:, cols] = emb.astype(F32) + mixed
        return 0

    lax.fori_loop(0, emb_ref.shape[1] // 128, pair, 0)


def attend(q_ref, k_ref, v_ref, out_ref, blk, low, high):
    masks = half_masks()
    rows = pl.ds(blk * 256, 256)
    span = pl.ds(blk * 256, 768)
    q = q_ref[rows, :]
    k = k_ref[span, :]
    v = v_ref[span, :]
    gap = lax.broadcasted_iota(jnp.int32, (256, 768), 1) - lax.broadcasted_iota(
        jnp.int32, (256, 768), 0
    )
    col = lax.broadcasted_iota(jnp.int32, (256, 768), 1)
    live = (gap >= 0) & (gap <= 512) & (col >= low) & (col < high)
    total = None
    for n in range(2):
        score = jnp.where(live, nt(q * masks[n], k), -jnp.inf)
        top = jnp.max(score, axis=1, keepdims=True)
        term = jnp.exp(score - top)
        part = nn(term.astype(BF), v * masks[n]) / jnp.sum(term, axis=1, keepdims=True)
        total = part if total is None else total + part
    out_ref[rows, :] = total.astype(BF)


def encode_kernel(grid_ref, emb_ref, src_ref, len_ref, wkv_ref, gain_ref, hid_ref, norm_ref):
    encode(grid_ref, emb_ref, src_ref, len_ref, wkv_ref, hid_ref)
    unit, _ = norm_rows(hid_ref[...])
    norm_ref[...] = (unit * gain_ref[...]).astype(BF)


def attend_kernel(q_ref, k_ref, v_ref, out_ref):
    g = lax.axis_index("grp")
    for blk in range(4):
        low = jnp.where(g == 0, 256, 0) if blk == 0 else 0
        high = jnp.where(g == lax.axis_size("grp") - 1, 512, 768) if blk == 3 else 768
        attend(q_ref, k_ref, v_ref, out_ref, blk, low, high)


def head_sum():
    row = lax.broadcasted_iota(jnp.int32, (1024, 128), 0) // 64
    col = lax.broadcasted_iota(jnp.int32, (1024, 128), 1)
    return (row == col).astype(F32).astype(BF)


def head_spread():
    row = lax.broadcasted_iota(jnp.int32, (128, 1024), 0)
    col = lax.broadcasted_iota(jnp.int32, (128, 1024), 1) // 64
    return (row == col).astype(F32).astype(BF)


def decode(grid_ref, dfc_ref, srct_ref, src_ref, wq_ref, wf_ref, u_ref, slot_ref, est_ref, back_ref, xe, kv, bg, rg):
    pts = 256
    lane = lax.broadcasted_iota(jnp.int32, (pts, 1024), 1)
    for e in range(3):
        pick = (srct_ref[:, e : e + 1] == lane).astype(F32).astype(BF)

        def gather(j, _):
            cols = pl.ds(pl.multiple_of(j * 256, 256), 256)
            xe[e * pts : (e + 1) * pts, cols] = nn(pick, slot_ref[:, cols]).astype(BF)
            return 0

        lax.fori_loop(0, 4, gather, 0)

    def project(j, _):
        cols = pl.ds(pl.multiple_of(j * 256, 256), 256)
        kv[:, cols] = nn(xe[...], u_ref[:, cols]).astype(BF)
        return 0

    lax.fori_loop(0, 8, project, 0)
    query = tn(grid_ref[...], wq_ref[...]).astype(BF)
    bg[...] = tn(dfc_ref[...], wf_ref[...])
    hsum = head_sum()
    spread = head_spread()
    qf = query.astype(F32)
    score, along = [], []
    for e in range(3):
        rows = slice(e * pts, (e + 1) * pts)
        score.append(nn((qf * kv[rows, :1024].astype(F32)).astype(BF), hsum) * SCALE)
        along.append(nn((bg[...] * kv[rows, 1024:].astype(F32)).astype(BF), hsum))
    top = jnp.maximum(jnp.maximum(score[0], score[1]), score[2])
    term = [jnp.exp(s - top) for s in score]
    total = term[0] + term[1] + term[2]
    weight = [t / total for t in term]
    mean = weight[0] * along[0] + weight[1] * along[1] + weight[2] * along[2]
    mix = jnp.zeros((pts, 1024), F32)
    for e in range(3):
        rows = slice(e * pts, (e + 1) * pts)
        wide = nn(weight[e].astype(BF), spread)
        mix += wide * kv[rows, 1024:].astype(F32)
        grad = nn((weight[e] * (along[e] - mean) * SCALE).astype(BF), spread)
        kv[rows, :1024] = (grad * qf).astype(BF)
        kv[rows, 1024:] = (wide * bg[...]).astype(BF)
    est_ref[...] = grid_ref[0:100, :].astype(F32) + nt(wf_ref[...], mix.astype(BF))

    def unproject(j, _):
        cols = pl.ds(pl.multiple_of(j * 256, 256), 256)
        rg[:, cols] = nt(kv[...], u_ref[cols, :]).astype(BF)
        return 0

    lax.fori_loop(0, 4, unproject, 0)

    def scatter(j, _):
        rows = pl.ds(pl.multiple_of(j * 128, 128), 128)
        sub = lax.broadcasted_iota(jnp.int32, (128, pts), 0) + j * 128
        pick = jnp.concatenate(
            [(src_ref[e : e + 1, :] == sub).astype(F32).astype(BF) for e in range(3)], axis=1
        )
        back_ref[rows, :] = nn(pick, rg[...]).astype(BF)
        return 0

    lax.fori_loop(0, 8, scatter, 0)


def with_halo(cells, width):
    count = lax.axis_size("grp")
    head = cells[:width]
    tail = cells[-width:]
    return jnp.concatenate(
        [
            lax.ppermute(tail, "grp", [(i, (i + 1) % count) for i in range(count - 1)]),
            cells,
            lax.ppermute(head, "grp", [((i + 1) % count, i) for i in range(count - 1)]),
        ],
        axis=0,
    )


VM = pl.BlockSpec(memory_space=pltpu.VMEM)


def body(
    grid_in, mesh_embed, enc_src, enc_len, enc_kv_weight, proc_gain, qkv_weight, out_weight,
    dec_gain, unpack, wq, wf, dec_send, dec_src, dforecast,
):
    params = pltpu.CompilerParams(vmem_limit_bytes=50 * 2**20)
    hidden, normed_in = pl.pallas_call(
        encode_kernel,
        out_shape=(
            jax.ShapeDtypeStruct((128, 1024), F32),
            jax.ShapeDtypeStruct((128, 1024), BF),
        ),
        in_specs=[VM] * 6,
        out_specs=(VM, VM),
        compiler_params=params,
    )(grid_in, mesh_embed, enc_src, enc_len.reshape(1, -1), enc_kv_weight, proc_gain.reshape(1, -1))
    triple = jnp.dot(
        lax.all_gather(normed_in, "head", axis=0, tiled=True),
        qkv_weight.reshape(1024, 384),
        preferred_element_type=F32,
    ).astype(BF)
    query = triple[:, :128] * SCALE
    extended = with_halo(triple[:, 128:], 256)
    attended = pl.pallas_call(
        attend_kernel,
        out_shape=jax.ShapeDtypeStruct((1024, 128), BF),
        in_specs=[VM] * 3,
        out_specs=VM,
        compiler_params=params,
    )(query, extended[:, :128], extended[:, 128:])
    projected = lax.psum_scatter(
        jnp.dot(attended, out_weight, preferred_element_type=F32).astype(BF),
        "head", scatter_dimension=0, tiled=True,
    ).astype(F32)
    unit, inverse = norm_rows(hidden + projected)
    dec_in = (unit * dec_gain).astype(BF)
    flat = dec_send.reshape(-1)
    pick = (flat[:, None] == jnp.arange(128)[None, :]).astype(BF)
    sent = jnp.dot(pick, dec_in, preferred_element_type=F32).astype(BF)
    arrived = lax.all_to_all(sent.reshape(32, 32, 1024), "grp", 0, 0, tiled=True).reshape(1024, 1024)
    estimated, back = pl.pallas_call(
        decode,
        out_shape=(
            jax.ShapeDtypeStruct((100, 256), F32),
            jax.ShapeDtypeStruct((1024, 1024), BF),
        ),
        in_specs=[VM] * 8,
        out_specs=(VM, VM),
        scratch_shapes=[
            pltpu.VMEM((768, 1024), BF),
            pltpu.VMEM((768, 2048), BF),
            pltpu.VMEM((256, 1024), F32),
            pltpu.VMEM((768, 1024), BF),
        ],
        compiler_params=params,
    )(grid_in, dforecast, dec_src.T, dec_src, wq, wf, unpack, arrived)
    returned = lax.all_to_all(back.reshape(32, 32, 1024), "grp", 0, 0, tiled=True).reshape(1024, 1024)
    place = (jnp.arange(128)[:, None] == flat[None, :]).astype(BF)
    entry = jnp.dot(place, returned, preferred_element_type=F32)
    scaled = entry * dec_gain
    first = jnp.mean(scaled, axis=-1, keepdims=True)
    second = jnp.mean(scaled * unit, axis=-1, keepdims=True)
    return estimated, inverse * (scaled - first - unit * second)


def solution(mesh):
    return jax.shard_map(
        body,
        mesh=mesh,
        in_specs=(
            P(None, ("grp", "head")), P(("grp", "head"), None), P(None, ("grp", "head")),
            P(("grp", "head")), P(), P(), P(None, None, "head"), P("head", None), P(), P(), P(), P(),
            P(("grp", "head"), None), P(None, ("grp", "head")), P(None, ("grp", "head")),
        ),
        out_specs=(P(None, ("grp", "head")), P(("grp", "head"), None)),
        check_vma=False,
    )
```

time: 382 us -> 258 us (0.68); the launches traced: 376 us -> 257 us
  local copies, waits for them, and re-layouts: 81.9 us -> 6.61 us
  blocking collectives: 0 us -> 58.2 us
  other arithmetic: 51.3 us -> 3.33 us
  waiting for transfers between devices: 155 us -> 120 us
  matrix products: 41.3 us -> 8.55 us
  Pallas kernels: 0 us -> 31.6 us
  loops' own time: 8.49 us -> 0 us
  starting transfers between devices: 23 us -> 15.2 us
    all_to_all x0 -> x1, blocking collectives: none -> 58.2 us  [body(): lax.all_to_all(back.reshape(32, 32, 1024), 'grp', 0, 0, tiled=True)]
    all_to_all x2 -> x1, waiting for transfers between devices: 85.3 us -> 51.1 us  [body(): lax.all_to_all(sent.reshape(32, 32, 1024), 'grp', 0, 0, tiled=True)]
    pallas_call x0 -> x3, Pallas kernels: none -> 31.6 us  [the longest x1 22 us: body(): pl.pallas_call(decode, out_shape=(jax.ShapeDtypeStruct((100, 256), F32),...]
    scatter-add x2 -> x0, other arithmetic: 28.4 us -> none  [the longest x1 18.6 us: readout_tile(): jax.ops.segment_sum(edge_grad.reshape(fan_in * point_count, 2 * entry_ext...]
    gather x3 -> x0, local copies, waits for them, and re-layouts: 26.3 us -> none  [the longest x1 11 us: encode_block(): edge_rows = grid_kv[sender_vertices]]
    dot_general x10 -> x4, matrix products: 34.2 us -> 8.55 us  [the longest x1 3.07 us: body(): sent = jnp.dot(pick, dec_in, preferred_element_type=F32).astype(BF)]
    unnamed x41 -> x32, local copies, waits for them, and re-layouts: 21.5 us -> 6.43 us
    mul x6 -> x0, local copies, waits for them, and re-layouts: 12.4 us -> none  [the longest x3 6.2 us: readout_tile(): score_grad[..., None] * query_heads.astype(jnp.float32) * score_scale]
  transfers between devices with their start and end apart: 6 -> 5, of which waited for: 6 -> 5; matrix products, arithmetic and copies ran while one was open for 4% -> 1% of each run, Pallas kernels for 0% -> 0%
where the time goes in v1:
time: 258 us; the launch traced here: 257 us
  waiting for transfers between devices  120 us (47%)
  blocking collectives  58.2 us (23%)
  Pallas kernels  31.6 us (12%)
  starting transfers between devices  15.2 us (6%)
  between operations  14.2 us (6%)
  matrix products  8.55 us (3%)
  local copies, waits for them, and re-layouts  6.61 us (3%)
  other arithmetic  3.33 us (1%)
    all_to_all x1, blocking collectives, body(): lax.all_to_all(back.reshape(32, 32, 1024), 'grp', 0, 0, tiled=True)  58.2 us
    all_to_all x1, waiting for transfers between devices, body(): lax.all_to_all(sent.reshape(32, 32, 1024), 'grp', 0, 0, tiled=True)  51.1 us
    reduce_scatter x1, waiting for transfers between devices, body(): lax.psum_scatter(jnp.dot(attended, out_weight, preferred_element_type=F32...  34.5 us
    all_gather x1, waiting for transfers between devices, body(): lax.all_gather(normed_in, 'head', axis=0, tiled=True)  28.1 us
    pallas_call x1, Pallas kernels, body(): pl.pallas_call(decode, out_shape=(jax.ShapeDtypeStruct((100, 256), F32),...  22 us
    all_to_all x1, starting transfers between devices, body(): lax.all_to_all(sent.reshape(32, 32, 1024), 'grp', 0, 0, tiled=True)  10.3 us
    unnamed x32, local copies, waits for them, and re-layouts  6.43 us
    pallas_call x1, Pallas kernels, body(): pl.pallas_call(encode_kernel, out_shape=(jax.ShapeDtypeStruct((128, 1024)...  6.21 us
  transfers between devices with their start and end apart: 5, of which 5 were waited for; matrix products, arithmetic and copies ran while one was open for 1% of the time, Pallas kernels for 0%

profile of v1, /device:TPU:24, one launch (start us, length us, event | category | flops | bytes accessed | tf_op | source)
XLA Modules:
  0.0 257.3 jit_solution(11334497334603181395)
XLA Ops:
  7.2 0.0 all-gather.2.cloned.1.call-start
  7.2 1.0 copy-done.1
  8.3 0.9 copy-done.2
  9.2 0.8 copy-done.3
  10.1 0.7 copy-done.9
  10.7 0.7 copy-done.10
  11.4 0.7 copy-done.11
  12.1 6.2 %shard_map.158 = (f32[128,1024]{1,0:T(8,128)S(1)}, bf16[128,1024]{1,0:T(8,128)(2,1)}) custom-call(bf16[112,256]{1,0:T(8,128)(2,1)S(1)} %copy-done.3, bf16[128,1024]{1,0:T(8,128)(2,1)S(1)} %copy-done.2, s32[16,128]{1,0:T(8,128)S(1)} %copy-done.9, s32[1,128]{1,0:T(1,128)S(1)} %bitcast.16, bf16[112,2048]{1,0:T(8,128)(2,1)S(1)} %copy-done.1, f32[1,1024]{1,0:T(1,128)S(1)} %bitcast.15), custom_call_target="tpu_custom_call" | custom-call | tf_op jit(solution)/shard_map/pallas_call | solution.py:204
  18.3 0.0 reduce-scatter.2.cloned.1.call-start
  18.4 1.4 copy.19
  19.8 28.1 %all-gather.2.cloned.1.call-done = bf16[1024,1024]{1,0:T(8,128)(2,1)} async-done(((bf16[128,1024]{1,0:T(8,128)(2,1)}), bf16[1024,1024]{1,0:T(8,128)(2,1)}) %all-gather.2.cloned.1.call-update) | async-done | bytes 2097168 | tf_op jit(solution)/shard_map/all_gather | solution.py:215
  47.9 2.9 %convolution_convert_fusion.2 = bf16[1024,384]{1,0:T(8,128)(2,1)S(1)} fusion(bf16[1024,1024]{1,0:T(8,128)(2,1)} %all-gather.2.cloned.1.call-done, bf16[1024,384]{0,1:T(8,128)(2,1)S(1)} %bitcast.18), kind=kOutput, calls=%fused_computation.2 | convolution fusion | flops 805699584 | bytes 3670016 | tf_op jit(solution)/shard_map/dot_general | solution.py:214
  50.8 3.5 %collective-permute-start = (bf16[256,256]{1,0:T(8,128)(2,1)S(1)}, bf16[256,256]{1,0:T(8,128)(2,1)S(1)}, u32[]{:S(2)}, u32[]{:S(2)}) collective-permute-start(bf16[256,256]{1,0:T(8,128)(2,1)S(1)} %get-tuple-element.14), channel_id=1, source_target_pairs={{0,8},{8,16},{16,24},{24,32},{32,40},{40,48},{48,56},{56,64},{64,7... | collective-permute-start | bytes 393224 | tf_op jit(solution)/shard_map/ppermute | solution.py:188
  54.3 1.3 collective-permute-start.1
  55.7 1.8 collective-permute-done
  57.4 4.1 %collective-permute-done.1 = bf16[256,256]{1,0:T(8,128)(2,1)S(1)} collective-permute-done((bf16[256,256]{1,0:T(8,128)(2,1)S(1)}, bf16[256,256]{1,0:T(8,128)(2,1)S(1)}, u32[]{:S(2)}, u32[]{:S(2)}) %collective-permute-start.1) | collective-permute-done | bytes 131104 | tf_op jit(solution)/shard_map/ppermute | solution.py:190
  61.6 0.1 pad_maximum_fusion
  61.6 0.1 fusion.7
  61.7 3.4 %shard_map.159 = bf16[1024,128]{1,0:T(8,128)(2,1)S(1)} custom-call(bf16[1024,128]{1,0:T(8,128)(2,1)S(1)} %slice_multiply_fusion.q_ref, bf16[1536,128]{1,0:T(8,128)(2,1)S(1)} %get-tuple-element.13.k_ref, bf16[1536,128]{1,0:T(8,128)(2,1)S(1)} %get-tuple-element.12.v_ref), custom_call_target="tpu_custom_call" | custom-call | tf_op jit(solution)/shard_map/pallas_call | solution.py:221
  65.1 2.0 convolution_convert_fusion.1
  67.1 0.1 eq.28
  67.2 34.5 %reduce-scatter.2.cloned.1.call-done = bf16[128,1024]{1,0:T(8,128)(2,1)} async-done(((bf16[1024,1024]{1,0:T(8,128)(2,1)}), bf16[128,1024]{1,0:T(8,128)(2,1)}) %reduce-scatter.2.cloned.1.call-update) | async-done | bytes 262160 | tf_op jit(solution)/shard_map/reduce_scatter | solution.py:228
  101.7 1.1 fusion.5
  102.7 1.1 multiply_reduce_fusion.1
  103.9 3.1 %convolution_convert_fusion = bf16[1024,1024]{1,0:T(8,128)(2,1)} fusion(f32[1024]{0:T(1024)S(1)} %copy-done.13, f32[128]{0:T(128)S(1)} %add_rsqrt_fusion, f32[128]{0:T(128)S(1)} %broadcast_multiply_fusion.2, s32[1024]{0:T(1024)S(1)} %eq.28, f32[128,1024]{1,0:T(8,128)S(1)} %get-tuple-element.6, bf16[128,1024]{1,0:T(8,128)(2,1)} %reduce-scatter.2.cloned.1.call-done), kind=kOutput, calls=%fused_computation | convolution fusion | flops 270401536 | bytes 2892800 | tf_op jit(solution)/shard_map/dot_general | solution.py:236
  107.0 10.3 %all-to-all-start = ((bf16[32,32,1024]{2,1,0:T(8,128)(2,1)}), bf16[32,32,1024]{2,1,0:T(8,128)(2,1)}, u32[]{:S(2)}, u32[]{:S(2)}) async-start(bf16[32,32,1024]{2,1,0:T(8,128)(2,1)} %bitcast.4), calls=%async_computation.1 | async-start | bytes 4194304 | tf_op jit(solution)/shard_map/all_to_all | solution.py:237
  117.3 0.1 copy.18
  117.5 51.1 %all-to-all-done = bf16[32,32,1024]{2,1,0:T(8,128)(2,1)} async-done(((bf16[32,32,1024]{2,1,0:T(8,128)(2,1)}), bf16[32,32,1024]{2,1,0:T(8,128)(2,1)}, u32[]{:S(2)}, u32[]{:S(2)}) %all-to-all-start) | async-done | bytes 2097184 | tf_op jit(solution)/shard_map/all_to_all | solution.py:237
  168.6 22.0 %shard_map.160 = (f32[100,256]{1,0:T(8,128)}, bf16[1024,1024]{1,0:T(8,128)(2,1)S(1)}) custom-call(bf16[112,256]{1,0:T(8,128)(2,1)S(1)} %copy-done.4, bf16[100,256]{1,0:T(8,128)(2,1)S(1)} %copy-done.7, s32[256,3]{1,0:T(8,128)S(1)} %bitcast.14, s32[3,256]{1,0:T(4,128)S(1)} %copy-done.8, bf16[112,1024]{1,0:T(8,128)(2,1)S(1)} %copy-done.5, ...), custom_call_target="tpu_custom_call" | custom-call | tf_op jit(solution)/shard_map/pallas_call | solution.py:238
  190.6 58.2 %all_to_all.10 = bf16[32,32,1024]{2,1,0:T(8,128)(2,1)S(1)} all-to-all(bf16[32,32,1024]{2,1,0:T(8,128)(2,1)S(1)} %bitcast.13), channel_id=1, replica_groups=mesh['grp'=32,'head'=8] {'grp'}, dimensions={0} | all-to-all | bytes 4194304 | tf_op jit(solution)/shard_map/all_to_all | solution.py:254
  248.8 0.6 fusion.6
  249.5 1.0 subtract_multiply_fusion
  (32 shorter events, 0.2 us)
Async XLA Ops:
  7.2 57.9 %copy-start = (bf16[128,1024]{1,0:T(8,128)(2,1)S(1)}, bf16[128,1024]{1,0:T(8,128)(2,1)}, u32[]{:S(2)}) copy-start(bf16[128,1024]{1,0:T(8,128)(2,1)} %param.22) | copy-start | bytes 786436
  7.2 40.7 %all-gather.2.cloned.1.call-start = ((), (), s32[]{:S(2)}) async-start(), calls=%async_computation.3 | async-start | bytes 2359296 | tf_op jit(solution)/shard_map/all_gather | solution.py:215
  7.2 1.1 copy-start.1
  8.3 0.9 copy-start.2
  9.2 0.8 copy-start.3
  10.1 0.7 copy-start.9
  10.7 0.7 copy-start.10
  11.4 0.7 copy-start.11
  18.3 83.3 %reduce-scatter.2.cloned.1.call-start = ((), (), s32[]{:S(2)}) async-start(), calls=%async_computation.4 | async-start | bytes 2359296 | tf_op jit(solution)/shard_map/reduce_scatter | solution.py:228
  50.8 6.6 %collective-permute-start = (bf16[256,256]{1,0:T(8,128)(2,1)S(1)}, bf16[256,256]{1,0:T(8,128)(2,1)S(1)}, u32[]{:S(2)}, u32[]{:S(2)}) collective-permute-start(bf16[256,256]{1,0:T(8,128)(2,1)S(1)} %get-tuple-element.14), channel_id=1, source_target_pairs={{0,8},{8,16},{16,24},{24,32},{32,40},{40,48},{48,56},{56,64},{64,7... | collective-permute-start | bytes 393224 | tf_op jit(solution)/shard_map/ppermute | solution.py:188
  54.3 7.2 %collective-permute-start.1 = (bf16[256,256]{1,0:T(8,128)(2,1)S(1)}, bf16[256,256]{1,0:T(8,128)(2,1)S(1)}, u32[]{:S(2)}, u32[]{:S(2)}) collective-permute-start(bf16[256,256]{1,0:T(8,128)(2,1)S(1)} %get-tuple-element.15), channel_id=1, source_target_pairs={{8,0},{16,8},{24,16},{32,24},{40,32},{48,40},{56,48},{64,56},{72,6... | collective-permute-start | bytes 393224 | tf_op jit(solution)/shard_map/ppermute | solution.py:190
  65.0 2.1 copy-start.14
  67.1 36.8 %copy-start.13 = (f32[1024]{0:T(1024)S(1)}, f32[1024]{0:T(1024)}, u32[]{:S(2)}) copy-start(f32[1024]{0:T(1024)} %param.23) | copy-start | bytes 12292
  107.0 10.3 %copy-start.8 = (s32[3,256]{1,0:T(4,128)S(1)}, s32[3,256]{1,0:T(4,128)}, u32[]{:S(2)}) copy-start(s32[3,256]{1,0:T(4,128)} %src_ref.3) | copy-start | bytes 9220
  107.0 61.6 %copy-start.4 = (bf16[112,256]{1,0:T(8,128)(2,1)S(1)}, bf16[112,256]{1,0:T(8,128)(2,1)}, u32[]{:S(2)}) copy-start(bf16[112,256]{1,0:T(8,128)(2,1)} %grid_ref.3) | copy-start | bytes 172036
  107.0 61.6 %copy-start.5 = (bf16[112,1024]{1,0:T(8,128)(2,1)S(1)}, bf16[112,1024]{1,0:T(8,128)(2,1)}, u32[]{:S(2)}) copy-start(bf16[112,1024]{1,0:T(8,128)(2,1)} %wq_ref.1) | copy-start | bytes 688132
  107.0 61.6 %copy-start.6 = (bf16[100,1024]{1,0:T(8,128)(2,1)S(1)}, bf16[100,1024]{1,0:T(8,128)(2,1)}, u32[]{:S(2)}) copy-start(bf16[100,1024]{1,0:T(8,128)(2,1)} %wf_ref.1) | copy-start | bytes 614404
  107.0 61.6 %copy-start.7 = (bf16[100,256]{1,0:T(8,128)(2,1)S(1)}, bf16[100,256]{1,0:T(8,128)(2,1)}, u32[]{:S(2)}) copy-start(bf16[100,256]{1,0:T(8,128)(2,1)} %dfc_ref.1) | copy-start | bytes 153604
  107.0 61.5 %all-to-all-start = ((bf16[32,32,1024]{2,1,0:T(8,128)(2,1)}), bf16[32,32,1024]{2,1,0:T(8,128)(2,1)}, u32[]{:S(2)}, u32[]{:S(2)}) async-start(bf16[32,32,1024]{2,1,0:T(8,128)(2,1)} %bitcast.4), calls=%async_computation.1 | async-start | bytes 4194304 | tf_op jit(solution)/shard_map/all_to_all | solution.py:237
  190.6 58.3 %copy-start.12 = (bf16[128,1024]{1,0:T(8,128)(2,1)S(1)}, bf16[128,1024]{1,0:T(8,128)(2,1)}, u32[]{:S(2)}) copy-start(bf16[128,1024]{1,0:T(8,128)(2,1)} %reduce-scatter.2.cloned.1.call-done) | copy-start | bytes 786436
Sparse Core Ops, SparseCore 0:
  18.4 29.4 all-gather.1
  67.2 34.3 reduce-scatter.1

commit v2 on v1

--- a/solution.py
+++ b/solution.py
@@ -90,18 +90,219 @@
     out_ref[rows, :] = total.astype(BF)
 
 
-def encode_kernel(grid_ref, emb_ref, src_ref, len_ref, wkv_ref, gain_ref, hid_ref, norm_ref):
-    encode(grid_ref, emb_ref, src_ref, len_ref, wkv_ref, hid_ref)
-    unit, _ = norm_rows(hid_ref[...])
-    norm_ref[...] = (unit * gain_ref[...]).astype(BF)
-
-
-def attend_kernel(q_ref, k_ref, v_ref, out_ref):
+MESH = pl.DeviceIdType.MESH
+
+
+class Ring:
+    def __init__(self, full, send, recv):
+        h = lax.axis_index("head")
+        y, c = h // 2, h % 2
+        self.full, self.send, self.recv, self.used = full, send, recv, []
+        self.own = h
+        self.up = ((y + 1) % 4) * 2 + c
+        self.dn = ((y + 3) % 4) * 2 + c
+        self.op = ((y + 2) % 4) * 2 + c
+        self.flip = 1 - 2 * c
+        self.sib = h + self.flip
+
+    def copy(self, block, start, size, to, sem, land):
+        view = self.full.at[pl.ds(block * 128 + start, size), :]
+        copy = pltpu.make_async_remote_copy(
+            src_ref=view, dst_ref=view, send_sem=self.send.at[sem], recv_sem=self.recv.at[land],
+            device_id={"head": to}, device_id_type=MESH,
+        )
+        copy.start()
+        self.used.append(copy)
+        return copy
+
+    def begin(self):
+        own = self.own
+        self.dn_a = self.copy(own, 0, 64, self.up, 0, 0)
+        self.up_b = self.copy(own, 64, 64, self.dn, 1, 3)
+        self.side = self.copy(own, 0, 128, self.sib, 4, 6)
+        self.dn_b = self.copy(own, 64, 64, self.up, 2, 1)
+        self.up_a = self.copy(own, 0, 64, self.dn, 3, 2)
+
+    def forward(self):
+        self.dn_a.wait_recv()
+        self.op_a = self.copy(self.dn, 0, 64, self.up, 5, 4)
+        self.side_dn_a = self.copy(self.dn, 0, 64, self.sib, 6, 7)
+        self.up_b.wait_recv()
+        self.op_b = self.copy(self.up, 64, 64, self.dn, 7, 5)
+        self.side_up_b = self.copy(self.up, 64, 64, self.sib, 8, 8)
+
+    def near(self):
+        self.dn_b.wait_recv()
+        self.side_dn_b = self.copy(self.dn, 64, 64, self.sib, 9, 9)
+        self.up_a.wait_recv()
+        self.side_up_a = self.copy(self.up, 0, 64, self.sib, 10, 10)
+
+    def far(self):
+        self.op_a.wait_recv()
+        self.side_op_a = self.copy(self.op, 0, 64, self.sib, 11, 11)
+        self.op_b.wait_recv()
+        self.side_op_b = self.copy(self.op, 64, 64, self.sib, 12, 12)
+
+    def finish(self):
+        for copy in self.used:
+            copy.wait_send()
+
+
+def front_kernel(
+    grid_h, emb_h, src_h, len_h, wkv_h, pgain_h, wqkv_h, wout_h, dgain_h,
+    unit_o, inv_o, din_o,
+    grid_v, emb_v, src_v, len_v, wkv_v, pgain_v, wqkv_v, dgain_v, hid, full, wfull, q, kx, vx, att, afull,
+    load, nsend, nrecv, wsend, wrecv, hsend, hrecv, asend, arecv,
+):
     g = lax.axis_index("grp")
-    for blk in range(4):
+    h = lax.axis_index("head")
+    groups = lax.axis_size("grp")
+    right, left = (g + 1) % groups, (g + groups - 1) % groups
+    pairs = [
+        (wout_h, wfull.at[pl.ds(h * 128, 128), :]), (grid_h, grid_v), (emb_h, emb_v), (src_h, src_v),
+        (len_h, len_v), (wkv_h, wkv_v), (pgain_h, pgain_v), (wqkv_h, wqkv_v), (dgain_h, dgain_v),
+    ]
+    loads = [pltpu.make_async_copy(s, d, load.at[i]) for i, (s, d) in enumerate(pairs)]
+    for copy in loads:
+        copy.start()
+    barrier = pltpu.get_barrier_semaphore()
+    for i in range(1, 8):
+        pl.semaphore_signal(barrier, inc=1, device_id={"head": (h + i) % 8}, device_id_type=MESH)
+    for other in (right, left):
+        pl.semaphore_signal(barrier, inc=1, device_id={"grp": other}, device_id_type=MESH)
+    pl.semaphore_wait(barrier, 9)
+    loads[0].wait()
+    weights = Ring(wfull, wsend, wrecv)
+    weights.begin()
+    for copy in loads[1:]:
+        copy.wait()
+
+    encode(grid_v, emb_v, src_v, len_v, wkv_v, hid)
+    unit, _ = norm_rows(hid[...])
+    full[pl.ds(h * 128, 128), :] = (unit * pgain_v[...]).astype(BF)
+    rows = Ring(full, nsend, nrecv)
+    rows.begin()
+
+    def project(block):
+        at = pl.multiple_of(block * 128, 128)
+        triple = nn(full[pl.ds(at, 128), :], wqkv_v[...]).astype(BF)
+        q[pl.ds(at, 128), :] = (triple[:, :128].astype(F32) * SCALE).astype(BF)
+        kx[pl.ds(at + 256, 128), :] = triple[:, 128:256]
+        vx[pl.ds(at + 256, 128), :] = triple[:, 256:]
+
+    flip = rows.flip
+    project(h)
+    rows.side.wait_recv()
+    project(rows.sib)
+    rows.forward()
+    rows.near()
+    project(rows.dn)
+    project(rows.up)
+    rows.side_dn_a.wait_recv()
+    rows.side_dn_b.wait_recv()
+    project(rows.dn + flip)
+    rows.side_up_a.wait_recv()
+    rows.side_up_b.wait_recv()
+    project(rows.up + flip)
+    rows.far()
+    project(rows.op)
+    rows.side_op_a.wait_recv()
+    rows.side_op_b.wait_recv()
+    project(rows.op + flip)
+
+    halos = []
+    for i, ref in enumerate((kx, vx)):
+        for j, (start, land, to) in enumerate(((1024, 0, right), (256, 1280, left))):
+            copy = pltpu.make_async_remote_copy(
+                src_ref=ref.at[pl.ds(start, 256), :], dst_ref=ref.at[pl.ds(land, 256), :],
+                send_sem=hsend.at[i * 2 + j], recv_sem=hrecv.at[i * 2 + j],
+                device_id={"grp": to}, device_id_type=MESH,
+            )
+            copy.start()
+            halos.append(copy)
+    weights.forward()
+    weights.near()
+
+    def give(to):
+        return pltpu.make_async_remote_copy(
+            src_ref=att.at[pl.ds(to * 128, 128), :],
+            dst_ref=afull.at[:, pl.ds(pl.multiple_of(h * 128, 128), 128)],
+            send_sem=asend.at[to], recv_sem=arecv.at[h],
+            device_id={"head": to}, device_id_type=MESH,
+        )
+
+    for blk in (1, 2, 0, 3):
+        if blk == 0:
+            for copy in halos:
+                copy.wait_recv()
         low = jnp.where(g == 0, 256, 0) if blk == 0 else 0
-        high = jnp.where(g == lax.axis_size("grp") - 1, 512, 768) if blk == 3 else 768
-        attend(q_ref, k_ref, v_ref, out_ref, blk, low, high)
+        high = jnp.where(g == groups - 1, 512, 768) if blk == 3 else 768
+        attend(q, kx, vx, att, blk, low, high)
+        for to in (2 * blk, 2 * blk + 1):
+
+            @pl.when(to != h)
+            def _():
+                give(to).start()
+
+    weights.far()
+    mine = pl.multiple_of(h * 128, 128)
+    afull[:, pl.ds(mine, 128)] = att[pl.ds(mine, 128), :]
+    for copy in (
+        weights.side, weights.side_dn_a, weights.side_dn_b, weights.side_up_a, weights.side_up_b,
+        weights.side_op_a, weights.side_op_b,
+    ):
+        copy.wait_recv()
+    for other in range(8):
+
+        @pl.when(other != h)
+        def _():
+            pltpu.make_async_remote_copy(
+                src_ref=att.at[pl.ds(0, 128), :],
+                dst_ref=afull.at[:, pl.ds(other * 128, 128)],
+                send_sem=asend.at[other], recv_sem=arecv.at[other],
+                device_id={"head": other}, device_id_type=MESH,
+            ).wait()
+
+    state = hid[...] + nn(afull[...], wfull[...])
+    unit, inverse = norm_rows(state)
+    unit_o[...] = unit
+    inv_o[...] = jnp.broadcast_to(inverse, (128, 128))
+    din_o[...] = (unit * dgain_v[...]).astype(BF)
+    rows.finish()
+    weights.finish()
+    for copy in halos:
+        copy.wait_send()
+
+
+def front(grid_in, mesh_embed, enc_src, enc_len, wkv, pgain, wqkv, wout, dgain):
+    ops = (grid_in, mesh_embed, enc_src, enc_len, wkv, pgain, wqkv)
+    stage = [pltpu.VMEM(a.shape, a.dtype) for a in ops] + [pltpu.VMEM(dgain.shape, F32)]
+    dma = pltpu.SemaphoreType.DMA
+    return pl.pallas_call(
+        front_kernel,
+        out_shape=(
+            jax.ShapeDtypeStruct((128, 1024), F32),
+            jax.ShapeDtypeStruct((128, 128), F32),
+            jax.ShapeDtypeStruct((128, 1024), BF),
+        ),
+        in_specs=[pl.BlockSpec(memory_space=pl.ANY)] * 9,
+        out_specs=(VM, VM, VM),
+        scratch_shapes=stage
+        + [
+            pltpu.VMEM((128, 1024), F32),
+            pltpu.VMEM((1024, 1024), BF),
+            pltpu.VMEM((1024, 1024), BF),
+            pltpu.VMEM((1024, 128), BF),
+            pltpu.VMEM((1536, 128), BF),
+            pltpu.VMEM((1536, 128), BF),
+            pltpu.VMEM((1024, 128), BF),
+            pltpu.VMEM((128, 1024), BF),
+            dma((9,)), dma((13,)), dma((13,)), dma((13,)), dma((13,)), dma((4,)), dma((4,)), dma((8,)), dma((8,)),
+        ],
+        compiler_params=pltpu.CompilerParams(
+            vmem_limit_bytes=60 * 2**20, collective_id=0, has_side_effects=True
+        ),
+    )(*ops, wout, dgain)
 
 
 def head_sum():
@@ -179,20 +380,6 @@
     lax.fori_loop(0, 8, scatter, 0)
 
 
-def with_halo(cells, width):
-    count = lax.axis_size("grp")
-    head = cells[:width]
-    tail = cells[-width:]
-    return jnp.concatenate(
-        [
-            lax.ppermute(tail, "grp", [(i, (i + 1) % count) for i in range(count - 1)]),
-            cells,
-            lax.ppermute(head, "grp", [((i + 1) % count, i) for i in range(count - 1)]),
-        ],
-        axis=0,
-    )
-
-
 VM = pl.BlockSpec(memory_space=pltpu.VMEM)
 
 
@@ -201,36 +388,11 @@
     dec_gain, unpack, wq, wf, dec_send, dec_src, dforecast,
 ):
     params = pltpu.CompilerParams(vmem_limit_bytes=50 * 2**20)
-    hidden, normed_in = pl.pallas_call(
-        encode_kernel,
-        out_shape=(
-            jax.ShapeDtypeStruct((128, 1024), F32),
-            jax.ShapeDtypeStruct((128, 1024), BF),
-        ),
-        in_specs=[VM] * 6,
-        out_specs=(VM, VM),
-        compiler_params=params,
-    )(grid_in, mesh_embed, enc_src, enc_len.reshape(1, -1), enc_kv_weight, proc_gain.reshape(1, -1))
-    triple = jnp.dot(
-        lax.all_gather(normed_in, "head", axis=0, tiled=True),
-        qkv_weight.reshape(1024, 384),
-        preferred_element_type=F32,
-    ).astype(BF)
-    query = triple[:, :128] * SCALE
-    extended = with_halo(triple[:, 128:], 256)
-    attended = pl.pallas_call(
-        attend_kernel,
-        out_shape=jax.ShapeDtypeStruct((1024, 128), BF),
-        in_specs=[VM] * 3,
-        out_specs=VM,
-        compiler_params=params,
-    )(query, extended[:, :128], extended[:, 128:])
-    projected = lax.psum_scatter(
-        jnp.dot(attended, out_weight, preferred_element_type=F32).astype(BF),
-        "head", scatter_dimension=0, tiled=True,
-    ).astype(F32)
-    unit, inverse = norm_rows(hidden + projected)
-    dec_in = (unit * dec_gain).astype(BF)
+    unit, inverse, dec_in = front(
+        grid_in, mesh_embed, enc_src, enc_len.reshape(1, -1), enc_kv_weight, proc_gain.reshape(1, -1),
+        qkv_weight.reshape(1024, 384), out_weight, dec_gain.reshape(1, -1),
+    )
+    inverse = inverse[:, :1]
     flat = dec_send.reshape(-1)
     pick = (flat[:, None] == jnp.arange(128)[None, :]).astype(BF)
     sent = jnp.dot(pick, dec_in, preferred_element_type=F32).astype(BF)

time: 258 us -> 186 us (0.72)
  blocking collectives: 58.2 us -> 0 us
  Pallas kernels: 31.6 us -> 64 us
  waiting for transfers between devices: 120 us -> 100 us
  between operations: 14.2 us -> 0.73 us
  matrix products: 8.55 us -> 3.59 us
  starting transfers between devices: 15.2 us -> 11.6 us
    all_to_all x1 -> x0, blocking collectives: 58.2 us -> none  [body(): lax.all_to_all(back.reshape(32, 32, 1024), 'grp', 0, 0, tiled=True)]
    all_to_all x0 -> x1, waiting for transfers between devices: none -> 49.9 us  [body(): lax.all_to_all(back.reshape(32, 32, 1024), 'grp', 0, 0, tiled=True)]
    reduce_scatter x1 -> x0, waiting for transfers between devices: 34.5 us -> none  [body(): lax.psum_scatter(jnp.dot(attended, out_weight, preferred_element_type=F32...]
    pallas_call x2 -> x1, Pallas kernels: 9.56 us -> 40.9 us  [front(): pl.pallas_call(front_kernel, out_shape=(jax.ShapeDtypeStruct((128, 1024),...]
    all_gather x1 -> x0, waiting for transfers between devices: 28.1 us -> none  [body(): lax.all_gather(normed_in, 'head', axis=0, tiled=True)]
    all_to_all x0 -> x1, starting transfers between devices: none -> 6.37 us  [body(): lax.all_to_all(back.reshape(32, 32, 1024), 'grp', 0, 0, tiled=True)]
    ppermute x2 -> x0, waiting for transfers between devices: 5.9 us -> none  [the longest x1 4.12 us: with_halo(): lax.ppermute(head, 'grp', [((i + 1) % count, i) for i in range(count - 1)])]
    all_to_all x1, starting transfers between devices: 10.3 us -> 5.2 us  [body(): lax.all_to_all(sent.reshape(32, 32, 1024), 'grp', 0, 0, tiled=True)]
  transfers between devices with their start and end apart: 5 -> 2, of which waited for: 5 -> 2; matrix products, arithmetic and copies ran while one was open for 1% -> 0% of each run, Pallas kernels for 0% -> 0%
where the time goes in v2:
time: 186 us
  waiting for transfers between devices  100 us (54%)
  Pallas kernels  64 us (34%)
  starting transfers between devices  11.6 us (6%)
  local copies, waits for them, and re-layouts  4.93 us (3%)
  matrix products  3.59 us (2%)
    all_to_all x1, waiting for transfers between devices, body(): lax.all_to_all(sent.reshape(32, 32, 1024), 'grp', 0, 0, tiled=True)  50.1 us
    all_to_all x1, waiting for transfers between devices, body(): lax.all_to_all(back.reshape(32, 32, 1024), 'grp', 0, 0, tiled=True)  49.9 us
    pallas_call x1, Pallas kernels, front(): pl.pallas_call(front_kernel, out_shape=(jax.ShapeDtypeStruct((128, 1024),...  40.9 us
    pallas_call x1, Pallas kernels, body(): pl.pallas_call(decode, out_shape=(jax.ShapeDtypeStruct((100, 256), F32),...  23.1 us
    all_to_all x1, starting transfers between devices, body(): lax.all_to_all(back.reshape(32, 32, 1024), 'grp', 0, 0, tiled=True)  6.37 us
    all_to_all x1, starting transfers between devices, body(): lax.all_to_all(sent.reshape(32, 32, 1024), 'grp', 0, 0, tiled=True)  5.2 us
  transfers between devices with their start and end apart: 2, of which 2 were waited for; matrix products, arithmetic and copies ran while one was open for 0% of the time, Pallas kernels for 0%

profile of v2, /device:TPU:24, one launch (start us, length us, event | category | flops | bytes accessed | tf_op | source)
XLA Modules:
  0.0 185.7 jit_solution(4697536580270426188)
XLA Ops:
  0.6 0.8 eq.28
  1.4 1.4 copy.20
  2.8 1.2 copy.21.wqkv_h
  4.0 40.9 %shard_map.158 = (f32[128,1024]{1,0:T(8,128)}, f32[128,128]{1,0:T(8,128)}, bf16[128,1024]{1,0:T(8,128)(2,1)}) custom-call(bf16[112,256]{1,0:T(8,128)(2,1)} %grid_ref.1, bf16[128,1024]{1,0:T(8,128)(2,1)} %emb_h.1, s32[16,128]{1,0:T(8,128)} %src_h.1, s32[1,128]{1,0:T(1,128)} %bitcast.18, bf16[112,2048]{1,0:T(8,128)(2,1)} %wkv_h.1, f32[1,1024]{1,0:T(1,128)} %bitcast.17, ...), custom_call_target="tpu_custom_call" | custom-call | tf_op jit(solution)/shard_map/pallas_call | solution.py:281
  44.9 3.0 %convolution_convert_fusion = bf16[1024,1024]{1,0:T(8,128)(2,1)} fusion(bf16[128,1024]{1,0:T(8,128)(2,1)} %get-tuple-element.7, s32[1024]{0:T(1024)S(1)} %eq.28), kind=kOutput, calls=%fused_computation | convolution fusion | flops 269615104 | bytes 2363392 | tf_op jit(solution)/shard_map/dot_general | solution.py:398
  47.9 0.0 copy-start.4
  47.9 0.0 copy-start
  47.9 0.0 copy-start.1
  47.9 0.0 copy-start.2
  47.9 0.0 copy-start.3
  47.9 5.2 %all-to-all-start = ((bf16[32,32,1024]{2,1,0:T(8,128)(2,1)}), bf16[32,32,1024]{2,1,0:T(8,128)(2,1)S(1)}, u32[]{:S(2)}, u32[]{:S(2)}) async-start(bf16[32,32,1024]{2,1,0:T(8,128)(2,1)} %bitcast.14), calls=%async_computation | async-start | bytes 4194304 | tf_op jit(solution)/shard_map/all_to_all | solution.py:399
  53.1 0.0 copy-done.4
  53.1 0.1 copy.19
  53.3 50.1 %all-to-all-done = bf16[32,32,1024]{2,1,0:T(8,128)(2,1)S(1)} async-done(((bf16[32,32,1024]{2,1,0:T(8,128)(2,1)}), bf16[32,32,1024]{2,1,0:T(8,128)(2,1)S(1)}, u32[]{:S(2)}, u32[]{:S(2)}) %all-to-all-start) | async-done | bytes 2097184 | tf_op jit(solution)/shard_map/all_to_all | solution.py:399
  103.4 0.0 copy-start.5
  103.4 1.3 copy-done.5
  104.7 0.0 copy-done
  104.7 0.0 copy-done.1
  104.7 0.0 copy-done.2
  104.7 0.0 copy-done.3
  104.7 23.1 %shard_map.159 = (f32[100,256]{1,0:T(8,128)}, bf16[1024,1024]{1,0:T(8,128)(2,1)}) custom-call(bf16[112,256]{1,0:T(8,128)(2,1)S(1)} %copy-done, bf16[100,256]{1,0:T(8,128)(2,1)S(1)} %copy-done.3, s32[256,3]{1,0:T(8,128)S(1)} %bitcast.11, s32[3,256]{1,0:T(4,128)S(1)} %copy-done.4, bf16[112,1024]{1,0:T(8,128)(2,1)S(1)} %copy-done.1, ...), custom_call_target="tpu_custom_call" | custom-call | tf_op jit(solution)/shard_map/pallas_call | solution.py:400
  127.8 0.0 copy-start.7
  127.8 0.0 copy-start.6
  127.8 0.0 copy-start.8
  127.8 6.4 %all-to-all-start.1 = ((bf16[32,32,1024]{2,1,0:T(8,128)(2,1)}), bf16[32,32,1024]{2,1,0:T(8,128)(2,1)S(1)}, u32[]{:S(2)}, u32[]{:S(2)}) async-start(bf16[32,32,1024]{2,1,0:T(8,128)(2,1)} %bitcast.7), calls=%async_computation.1 | async-start | bytes 4194304 | tf_op jit(solution)/shard_map/all_to_all | solution.py:416
  134.2 0.0 copy-done.7
  134.2 0.1 slice_reduce_fusion
  134.3 49.9 %all-to-all-done.1 = bf16[32,32,1024]{2,1,0:T(8,128)(2,1)S(1)} async-done(((bf16[32,32,1024]{2,1,0:T(8,128)(2,1)}), bf16[32,32,1024]{2,1,0:T(8,128)(2,1)S(1)}, u32[]{:S(2)}, u32[]{:S(2)}) %all-to-all-start.1) | async-done | bytes 2097184 | tf_op jit(solution)/shard_map/all_to_all | solution.py:416
  184.2 0.0 copy-done.6
  184.2 0.0 copy-done.8
  184.2 0.5 fusion.2
  184.8 0.9 subtract_multiply_fusion
  (1 shorter events, 0.0 us)
Async XLA Ops:
  47.9 5.2 %copy-start.4 = (s32[3,256]{1,0:T(4,128)S(1)}, s32[3,256]{1,0:T(4,128)}, u32[]{:S(2)}) copy-start(s32[3,256]{1,0:T(4,128)} %src_ref.1) | copy-start | bytes 9220
  47.9 56.8 %copy-start = (bf16[112,256]{1,0:T(8,128)(2,1)S(1)}, bf16[112,256]{1,0:T(8,128)(2,1)}, u32[]{:S(2)}) copy-start(bf16[112,256]{1,0:T(8,128)(2,1)} %grid_ref.1) | copy-start | bytes 172036
  47.9 56.8 %copy-start.1 = (bf16[112,1024]{1,0:T(8,128)(2,1)S(1)}, bf16[112,1024]{1,0:T(8,128)(2,1)}, u32[]{:S(2)}) copy-start(bf16[112,1024]{1,0:T(8,128)(2,1)} %wq_ref.1) | copy-start | bytes 688132
  47.9 56.8 %copy-start.2 = (bf16[100,1024]{1,0:T(8,128)(2,1)S(1)}, bf16[100,1024]{1,0:T(8,128)(2,1)}, u32[]{:S(2)}) copy-start(bf16[100,1024]{1,0:T(8,128)(2,1)} %wf_ref.1) | copy-start | bytes 614404
  47.9 56.8 %copy-start.3 = (bf16[100,256]{1,0:T(8,128)(2,1)S(1)}, bf16[100,256]{1,0:T(8,128)(2,1)}, u32[]{:S(2)}) copy-start(bf16[100,256]{1,0:T(8,128)(2,1)} %dfc_ref.1) | copy-start | bytes 153604
  47.9 55.4 %all-to-all-start = ((bf16[32,32,1024]{2,1,0:T(8,128)(2,1)}), bf16[32,32,1024]{2,1,0:T(8,128)(2,1)S(1)}, u32[]{:S(2)}, u32[]{:S(2)}) async-start(bf16[32,32,1024]{2,1,0:T(8,128)(2,1)} %bitcast.14), calls=%async_computation | async-start | bytes 4194304 | tf_op jit(solution)/shard_map/all_to_all | solution.py:399
  103.4 1.3 copy-start.5
  127.8 6.4 %copy-start.7 = (f32[128,128]{1,0:T(8,128)S(1)}, f32[128,128]{1,0:T(8,128)}, u32[]{:S(2)}) copy-start(f32[128,128]{1,0:T(8,128)} %get-tuple-element.9) | copy-start | bytes 196612
  127.8 56.4 %copy-start.6 = (f32[128,1024]{1,0:T(8,128)S(1)}, f32[128,1024]{1,0:T(8,128)}, u32[]{:S(2)}) copy-start(f32[128,1024]{1,0:T(8,128)} %get-tuple-element.11) | copy-start | bytes 1572868
  127.8 56.4 %copy-start.8 = (f32[1024]{0:T(1024)S(1)}, f32[1024]{0:T(1024)}, u32[]{:S(2)}) copy-start(f32[1024]{0:T(1024)} %param.23) | copy-start | bytes 12292
  127.8 56.4 %all-to-all-start.1 = ((bf16[32,32,1024]{2,1,0:T(8,128)(2,1)}), bf16[32,32,1024]{2,1,0:T(8,128)(2,1)S(1)}, u32[]{:S(2)}, u32[]{:S(2)}) async-start(bf16[32,32,1024]{2,1,0:T(8,128)(2,1)} %bitcast.7), calls=%async_computation.1 | async-start | bytes 4194304 | tf_op jit(solution)/shard_map/all_to_all | solution.py:416

commit v3 on v2

--- a/solution.py
+++ b/solution.py
@@ -317,7 +317,12 @@
     return (row == col).astype(F32).astype(BF)
 
 
-def decode(grid_ref, dfc_ref, srct_ref, src_ref, wq_ref, wf_ref, u_ref, slot_ref, est_ref, back_ref, xe, kv, bg, rg):
+def decode_ready(grid_ref, dfc_ref, wq_ref, wf_ref, query, bg):
+    query[...] = tn(grid_ref[...], wq_ref[...]).astype(BF)
+    bg[...] = tn(dfc_ref[...], wf_ref[...])
+
+
+def decode(grid_ref, srct_ref, wf_ref, u_ref, slot_ref, est_ref, xe, kv, query, bg, rg):
     pts = 256
     lane = lax.broadcasted_iota(jnp.int32, (pts, 1024), 1)
     for e in range(3):
@@ -336,11 +341,9 @@
         return 0
 
     lax.fori_loop(0, 8, project, 0)
-    query = tn(grid_ref[...], wq_ref[...]).astype(BF)
-    bg[...] = tn(dfc_ref[...], wf_ref[...])
     hsum = head_sum()
     spread = head_spread()
-    qf = query.astype(F32)
+    qf = query[...].astype(F32)
     score, along = [], []
     for e in range(3):
         rows = slice(e * pts, (e + 1) * pts)
@@ -368,16 +371,211 @@
 
     lax.fori_loop(0, 4, unproject, 0)
 
-    def scatter(j, _):
-        rows = pl.ds(pl.multiple_of(j * 128, 128), 128)
-        sub = lax.broadcasted_iota(jnp.int32, (128, pts), 0) + j * 128
+
+NX, NZ = 4, 8
+A, B = slice(0, 64), slice(64, 128)
+
+
+def back_kernel(
+    din_h, unit_h, inv_h, gain_h, tab_h, grid_h, dfc_h, srct_h, src_h, wq_h, wf_h, u_h,
+    est_o, vert_o,
+    unit_v, inv_v, gain_v, tab_v, grid_v, dfc_v, srct_v, src_v, wq_v, wf_v, u_v,
+    zbuf, tab, xs, arrived, xe, kv, query, bg, rg, bs, rback, outs, ins,
+    load, tsend, trecv, zsend, zrecv, xsend, xrecv, bsend, brecv, qsend, qrecv,
+):
+    g = lax.axis_index("grp")
+    x, z = g // NZ, g % NZ
+    nexts = [(z + 1) % NZ, (z + NZ - 1) % NZ]
+    pairs = [
+        (din_h, zbuf.at[z]), (tab_h, tab_v), (grid_h, grid_v), (dfc_h, dfc_v), (wq_h, wq_v), (wf_h, wf_v),
+        (srct_h, srct_v), (src_h, src_v), (u_h, u_v), (unit_h, unit_v), (inv_h, inv_v), (gain_h, gain_v),
+    ]
+    loads = [pltpu.make_async_copy(s, d, load.at[i]) for i, (s, d) in enumerate(pairs)]
+    for copy in loads:
+        copy.start()
+
+    def remote(source, target, send, recv, xx, zz):
+        copy = pltpu.make_async_remote_copy(
+            src_ref=source, dst_ref=target, send_sem=send, recv_sem=recv,
+            device_id={"grp": xx * NZ + zz}, device_id_type=MESH,
+        )
+        copy.start()
+        return copy
+
+    barrier = pltpu.get_barrier_semaphore()
+    for k in range(1, NZ):
+        pl.semaphore_signal(barrier, inc=1, device_id={"grp": x * NZ + (z + k) % NZ}, device_id_type=MESH)
+    for k in range(1, NX):
+        pl.semaphore_signal(barrier, inc=1, device_id={"grp": (x + k) % NX * NZ + z}, device_id_type=MESH)
+    pl.semaphore_wait(barrier, NX + NZ - 2)
+    loads[0].wait()
+    sent = []
+    ring = {}
+
+    def pass_on(way, d, chunk):
+        block = (z + d) % NZ if way else (z + NZ - d) % NZ
+        view = zbuf.at[block, pl.ds(64 * chunk, 64), :]
+        sem = way * 8 + d * 2 + chunk
+        ring[way, d, chunk] = remote(view, view, zsend.at[sem], zrecv.at[sem], x, nexts[way])
+        sent.append(ring[way, d, chunk])
+
+    hops = ((0, 0), (1, 1), (0, 1), (1, 0))
+    for way, chunk in hops:
+        pass_on(way, 0, chunk)
+    loads[1].wait()
+    tab[pl.ds(z, 1)] = tab_v[pl.ds(z, 1)]
+    tables = [
+        remote(tab_v.at[(z + k) % NZ], tab.at[z], tsend.at[k], trecv.at[k], x, (z + k) % NZ)
+        for k in range(1, NZ)
+    ]
+    sent.extend(tables)
+
+    def chosen(zz):
+        node = lax.broadcasted_iota(jnp.int32, (128, 128), 0)
+        return (node == tab[zz][0:1, :]).astype(F32).astype(BF)
+
+    crossing = []
+
+    def select(index, zz):
+        xs[index] = tn(chosen(zz), zbuf[zz]).astype(BF)
+        land = pl.ds(pl.multiple_of((x * NZ + zz) * 32, 32), 32)
+        for k in range(1, NX):
+            xx = (x + k) % NX
+            sem = index * NX + k
+            crossing.append(remote(
+                xs.at[index, pl.ds(pl.multiple_of(xx * 32, 32), 32), :], arrived.at[land, :],
+                xsend.at[sem], xrecv.at[sem], xx, z,
+            ))
+        arrived[land, :] = xs[index, pl.ds(pl.multiple_of(x * 32, 32), 32), :]
+
+    select(0, z)
+    for copy in loads[2:6]:
+        copy.wait()
+    decode_ready(grid_v, dfc_v, wq_v, wf_v, query, bg)
+    for copy in loads[6:]:
+        copy.wait()
+    for copy in tables:
+        copy.wait_recv()
+    for d in range(1, 5):
+        for way, chunk in hops:
+            last = way == chunk
+            if d < 4 or last:
+                ring[way, d - 1, chunk].wait_recv()
+            if d < 3 or (d == 3 and last):
+                pass_on(way, d, chunk)
+        if d < 4:
+            select(2 * d - 1, (z + NZ - d) % NZ)
+            select(2 * d, (z + d) % NZ)
+        else:
+            select(7, (z + 4) % NZ)
+    for copy in crossing:
+        copy.wait_recv()
+    decode(grid_v, srct_v, wf_v, u_v, arrived, est_o, xe, kv, query, bg, rg)
+
+    order = [(7, (z + 4) % NZ)]
+    for d in (3, 2, 1):
+        order += [(2 * d, (z + d) % NZ), (2 * d - 1, (z + NZ - d) % NZ)]
+    order.append((0, z))
+    returning = {}
+    for index, zz in order:
+        row = lax.broadcasted_iota(jnp.int32, (128, 256), 0)
+        slot = (row // 32 * NZ + zz) * 32 + row % 32
         pick = jnp.concatenate(
-            [(src_ref[e : e + 1, :] == sub).astype(F32).astype(BF) for e in range(3)], axis=1
+            [(src_v[e : e + 1, :] == slot).astype(F32).astype(BF) for e in range(3)], axis=1
         )
-        back_ref[rows, :] = nn(pick, rg[...]).astype(BF)
-        return 0
-
-    lax.fori_loop(0, 8, scatter, 0)
+        bs[index] = nn(pick, rg[...]).astype(BF)
+        land = pl.ds(pl.multiple_of(x * 32, 32), 32)
+        for k in range(1, NX):
+            xx = (x + k) % NX
+            sem = index * NX + k
+            returning[index, k] = remote(
+                bs.at[index, pl.ds(pl.multiple_of(xx * 32, 32), 32), :], rback.at[index, land, :],
+                bsend.at[sem], brecv.at[sem], xx, z,
+            )
+        rback[index, land, :] = bs[index, land, :]
+
+    def partial(index, zz):
+        for k in range(1, NX):
+            returning[index, k].wait_recv()
+        return nn(chosen(zz), rback[index])
+
+    flow = {}
+
+    def push(way, i, chunk):
+        rows = pl.ds(64 * chunk, 64)
+        sem = way * 8 + i * 2 + chunk
+        flow[way, i, chunk] = remote(
+            outs.at[way, i, rows, :], ins.at[way, i, rows, :], qsend.at[sem], qrecv.at[sem], x, nexts[way]
+        )
+
+    part = partial(7, (z + 4) % NZ)
+    outs[0, 3, A] = part[A].astype(BF)
+    push(0, 3, 0)
+    outs[1, 3, B] = part[B].astype(BF)
+    push(1, 3, 1)
+    for d in (3, 2, 1):
+        for way in range(2):
+            index = 2 * d - way
+            part = partial(index, (z + NZ - d) % NZ if way else (z + d) % NZ)
+            for chunk in (way, 1 - way):
+                rows = B if chunk else A
+                value = part[rows]
+                if d < 3 or chunk == way:
+                    flow[way, d, chunk].wait_recv()
+                    value = value + ins[way, d, rows].astype(F32)
+                outs[way, d - 1, rows] = value.astype(BF)
+                push(way, d - 1, chunk)
+    part = partial(0, z)
+    for way in range(2):
+        for chunk in range(2):
+            flow[way, 0, chunk].wait_recv()
+    grad = part + ins[0, 0].astype(F32) + ins[1, 0].astype(F32)
+    unit = unit_v[...]
+    scaled = grad * gain_v[...]
+    first = jnp.mean(scaled, axis=-1, keepdims=True)
+    second = jnp.mean(scaled * unit, axis=-1, keepdims=True)
+    vert_o[...] = inv_v[:, 0:1] * (scaled - first - unit * second)
+    for copy in sent + crossing + list(returning.values()) + list(flow.values()):
+        copy.wait_send()
+
+
+def back(din, unit, inv, gain, send, grid_in, dforecast, dec_src, wq, wf, u):
+    table = jnp.broadcast_to(
+        send.reshape(NX, NZ, 32).transpose(1, 0, 2).reshape(NZ, 1, 128), (NZ, 8, 128)
+    )
+    ops = (din, unit, inv, gain, table, grid_in, dforecast, dec_src.T, dec_src, wq, wf, u)
+    dma = pltpu.SemaphoreType.DMA
+    vm = pltpu.VMEM
+    return pl.pallas_call(
+        back_kernel,
+        out_shape=(
+            jax.ShapeDtypeStruct((100, 256), F32),
+            jax.ShapeDtypeStruct((128, 1024), F32),
+        ),
+        in_specs=[pl.BlockSpec(memory_space=pl.ANY)] * len(ops),
+        out_specs=(VM, VM),
+        scratch_shapes=[vm(a.shape, a.dtype) for a in ops[1:]]
+        + [
+            vm((NZ, 128, 1024), BF),
+            vm((NZ, 8, 128), jnp.int32),
+            vm((8, 128, 1024), BF),
+            vm((1024, 1024), BF),
+            vm((768, 1024), BF),
+            vm((768, 2048), BF),
+            vm((256, 1024), BF),
+            vm((256, 1024), F32),
+            vm((768, 1024), BF),
+            vm((8, 128, 1024), BF),
+            vm((8, 128, 1024), BF),
+            vm((2, 4, 128, 1024), BF),
+            vm((2, 4, 128, 1024), BF),
+            dma((12,)), dma((8,)), dma((8,)), dma((16,)), dma((16,)), dma((32,)), dma((32,)), dma((32,)), dma((32,)),
+            dma((16,)), dma((16,)),
+        ],
+        compiler_params=pltpu.CompilerParams(
+            vmem_limit_bytes=60 * 2**20, collective_id=1, has_side_effects=True
+        ),
+    )(*ops)
 
 
 VM = pl.BlockSpec(memory_space=pltpu.VMEM)
@@ -387,39 +585,13 @@
     grid_in, mesh_embed, enc_src, enc_len, enc_kv_weight, proc_gain, qkv_weight, out_weight,
     dec_gain, unpack, wq, wf, dec_send, dec_src, dforecast,
 ):
-    params = pltpu.CompilerParams(vmem_limit_bytes=50 * 2**20)
     unit, inverse, dec_in = front(
         grid_in, mesh_embed, enc_src, enc_len.reshape(1, -1), enc_kv_weight, proc_gain.reshape(1, -1),
         qkv_weight.reshape(1024, 384), out_weight, dec_gain.reshape(1, -1),
     )
-    inverse = inverse[:, :1]
-    flat = dec_send.reshape(-1)
-    pick = (flat[:, None] == jnp.arange(128)[None, :]).astype(BF)
-    sent = jnp.dot(pick, dec_in, preferred_element_type=F32).astype(BF)
-    arrived = lax.all_to_all(sent.reshape(32, 32, 1024), "grp", 0, 0, tiled=True).reshape(1024, 1024)
-    estimated, back = pl.pallas_call(
-        decode,
-        out_shape=(
-            jax.ShapeDtypeStruct((100, 256), F32),
-            jax.ShapeDtypeStruct((1024, 1024), BF),
-        ),
-        in_specs=[VM] * 8,
-        out_specs=(VM, VM),
-        scratch_shapes=[
-            pltpu.VMEM((768, 1024), BF),
-            pltpu.VMEM((768, 2048), BF),
-            pltpu.VMEM((256, 1024), F32),
-            pltpu.VMEM((768, 1024), BF),
-        ],
-        compiler_params=params,
-    )(grid_in, dforecast, dec_src.T, dec_src, wq, wf, unpack, arrived)
-    returned = lax.all_to_all(back.reshape(32, 32, 1024), "grp", 0, 0, tiled=True).reshape(1024, 1024)
-    place = (jnp.arange(128)[:, None] == flat[None, :]).astype(BF)
-    entry = jnp.dot(place, returned, preferred_element_type=F32)
-    scaled = entry * dec_gain
-    first = jnp.mean(scaled, axis=-1, keepdims=True)
-    second = jnp.mean(scaled * unit, axis=-1, keepdims=True)
-    return estimated, inverse * (scaled - first - unit * second)
+    return back(
+        dec_in, unit, inverse, dec_gain.reshape(1, -1), dec_send, grid_in, dforecast, dec_src, wq, wf, unpack
+    )
 
 
 def solution(mesh):

time: 186 us -> 134 us (0.72)
  waiting for transfers between devices: 100 us -> 0 us
  Pallas kernels: 64 us -> 126 us
  starting transfers between devices: 11.6 us -> 0 us
  matrix products: 3.59 us -> 0 us
  local copies, waits for them, and re-layouts: 4.93 us -> 7.53 us
    all_to_all x2 -> x0, waiting for transfers between devices: 100 us -> none  [the longest x1 50.1 us: body(): lax.all_to_all(sent.reshape(32, 32, 1024), 'grp', 0, 0, tiled=True)]
    pallas_call x1, Pallas kernels: 23.1 us -> 85.1 us  [back(): pl.pallas_call(back_kernel, out_shape=(jax.ShapeDtypeStruct((100, 256), F...]
    all_to_all x2 -> x0, starting transfers between devices: 11.6 us -> none  [the longest x1 6.37 us: body(): lax.all_to_all(back.reshape(32, 32, 1024), 'grp', 0, 0, tiled=True)]
    dot_general x2 -> x0, matrix products: 3.59 us -> none  [the longest x1 3.05 us: body(): sent = jnp.dot(pick, dec_in, preferred_element_type=F32).astype(BF)]
    unnamed x20 -> x8, local copies, waits for them, and re-layouts: 2.87 us -> 5.66 us
  transfers between devices with their start and end apart: 2 -> 0, of which waited for: 2 -> 0; matrix products, arithmetic and copies ran while one was open for 0% -> 0% of each run, Pallas kernels for 0% -> 0%
where the time goes in v3:
time: 134 us
  Pallas kernels  126 us (94%)
  local copies, waits for them, and re-layouts  7.53 us (6%)
    pallas_call x1, Pallas kernels, back(): pl.pallas_call(back_kernel, out_shape=(jax.ShapeDtypeStruct((100, 256), F...  85.1 us
    pallas_call x1, Pallas kernels, front(): pl.pallas_call(front_kernel, out_shape=(jax.ShapeDtypeStruct((128, 1024),...  40.8 us
    unnamed x8, local copies, waits for them, and re-layouts  5.66 us

profile of v3, /device:TPU:24, one launch (start us, length us, event | category | flops | bytes accessed | tf_op | source)
XLA Modules:
  0.0 134.1 jit_solution(7460079623132125398)
XLA Ops:
  0.6 0.0 copy-start
  0.6 0.0 copy-start.1
  0.7 1.4 %copy.20 = bf16[1024,3,128]{0,2,1:T(8,128)(2,1)S(1)} copy(bf16[1024,3,128]{2,0,1:T(8,128)(2,1)} %param.21) | data formatting | bytes 1572864 | tf_op args[6]
  2.1 1.2 copy.21.wqkv_h
  3.2 40.8 %shard_map.158 = (f32[128,1024]{1,0:T(8,128)}, f32[128,128]{1,0:T(8,128)}, bf16[128,1024]{1,0:T(8,128)(2,1)}) custom-call(bf16[112,256]{1,0:T(8,128)(2,1)} %grid_h.3, bf16[128,1024]{1,0:T(8,128)(2,1)} %emb_h.1, s32[16,128]{1,0:T(8,128)} %src_h.2, s32[1,128]{1,0:T(1,128)} %bitcast.14, bf16[112,2048]{1,0:T(8,128)(2,1)} %wkv_h.1, f32[1,1024]{1,0:T(1,128)} %bitcast.13, ...), custom_call_target="tpu_custom_call" | custom-call | tf_op jit(solution)/shard_map/pallas_call | solution.py:281
  44.1 0.0 copy-done
  44.1 0.8 copy.23
  44.9 0.0 copy-done.1
  44.9 0.1 broadcast_in_dim.7
  45.0 0.6 broadcast_in_dim.8.tab_h
  45.6 85.1 %shard_map.159 = (f32[100,256]{1,0:T(8,128)}, f32[128,1024]{1,0:T(8,128)}) custom-call(bf16[128,1024]{1,0:T(8,128)(2,1)} %get-tuple-element.5.din_h, f32[128,1024]{1,0:T(8,128)} %get-tuple-element.6.unit_h, f32[128,128]{1,0:T(8,128)} %get-tuple-element.7.inv_h, f32[1,1024]{1,0:T(1,128)} %bitcast.11, s32[8,8,128]{2,1,0:T(8,128)} %broadcast_in_dim.8.tab_h, ...), custom_call_target="tpu_custom_call" | custom-call | tf_op jit(solution)/shard_map/pallas_call | solution.py:549
  130.7 1.5 %copy.26 = f32[100,256]{1,0:T(8,128)} copy(f32[100,256]{1,0:T(8,128)} %get-tuple-element.10) | data formatting | bytes 204800
  132.2 1.9 %copy.27 = f32[128,1024]{1,0:T(8,128)} copy(f32[128,1024]{1,0:T(8,128)} %get-tuple-element.11) | data formatting | bytes 1048576
  (1 shorter events, 0.0 us)
Async XLA Ops:
  0.6 43.5 %copy-start = (s32[3,256]{1,0:T(4,128)S(1)}, s32[3,256]{1,0:T(4,128)}, u32[]{:S(2)}) copy-start(s32[3,256]{1,0:T(4,128)} %src_h.3) | copy-start | bytes 9220
  0.6 44.3 %copy-start.1 = (s32[32,32]{1,0:T(8,128)S(1)}, s32[32,32]{1,0:T(8,128)}, u32[]{:S(2)}) copy-start(s32[32,32]{1,0:T(8,128)} %param.27) | copy-start | bytes 12292

commit v4 on v2

v4 whole, which is shorter than its diff:
```python
import jax
import jax.numpy as jnp
from jax import lax
from jax.experimental import pallas as pl
from jax.experimental.pallas import tpu as pltpu
from jax.sharding import PartitionSpec as P

F32 = jnp.float32
BF = jnp.bfloat16
EPS = 1e-05
SCALE = 0.125


def nn(a, b):
    return lax.dot_general(a, b, (((1,), (0,)), ((), ())), preferred_element_type=F32)


def nt(a, b):
    return lax.dot_general(a, b, (((1,), (1,)), ((), ())), preferred_element_type=F32)


def tn(a, b):
    return lax.dot_general(a, b, (((0,), (0,)), ((), ())), preferred_element_type=F32)


def half_masks():
    lane = lax.broadcasted_iota(jnp.int32, (1, 128), 1)
    return [(lane < 64).astype(F32).astype(BF), (lane >= 64).astype(F32).astype(BF)]


def norm_rows(rows):
    row_mean = jnp.mean(rows, axis=-1, keepdims=True)
    centred = rows - row_mean
    spread = jnp.mean(centred * centred, axis=-1, keepdims=True)
    inverse = lax.rsqrt(spread + EPS)
    return centred * inverse, inverse


def encode(grid_ref, emb_ref, src_ref, len_ref, wkv_ref, hid_ref):
    points = grid_ref.shape[1]
    nodes = emb_ref.shape[0]
    pid = lax.broadcasted_iota(jnp.int32, (points, nodes), 0)
    count = jnp.zeros((points, nodes), F32)
    lens = len_ref[...]
    for e in range(src_ref.shape[0]):
        row = jnp.where(e < lens, src_ref[e : e + 1, :], -1)
        count += (pid == row).astype(F32)
    dead = jnp.where(count > 0, 0.0, -jnp.inf)
    grid_t = grid_ref[...].T
    masks = half_masks()

    def pair(j, _):
        cols = pl.ds(pl.multiple_of(j * 128, 128), 128)
        vcols = pl.ds(pl.multiple_of(j * 128 + 1024, 128), 128)
        keys = nn(grid_t, wkv_ref[:, cols]).astype(BF)
        values = nn(grid_t, wkv_ref[:, vcols]).astype(BF)
        emb = emb_ref[:, cols]
        weights = []
        for n in range(2):
            score = nt(keys, emb * masks[n]) * SCALE + dead
            top = jnp.max(score, axis=0, keepdims=True)
            term = jnp.exp(score - top) * count
            weights.append((term / jnp.sum(term, axis=0, keepdims=True)).astype(BF))
        mixed = tn(weights[0], values * masks[0]) + tn(weights[1], values * masks[1])
        hid_ref[:, cols] = emb.astype(F32) + mixed
        return 0

    lax.fori_loop(0, emb_ref.shape[1] // 128, pair, 0)


def attend(q_ref, k_ref, v_ref, out_ref, blk, low, high):
    masks = half_masks()
    rows = pl.ds(blk * 256, 256)
    span = pl.ds(blk * 256, 768)
    q = q_ref[rows, :]
    k = k_ref[span, :]
    v = v_ref[span, :]
    gap = lax.broadcasted_iota(jnp.int32, (256, 768), 1) - lax.broadcasted_iota(
        jnp.int32, (256, 768), 0
    )
    col = lax.broadcasted_iota(jnp.int32, (256, 768), 1)
    live = (gap >= 0) & (gap <= 512) & (col >= low) & (col < high)
    total = None
    for n in range(2):
        score = jnp.where(live, nt(q * masks[n], k), -jnp.inf)
        top = jnp.max(score, axis=1, keepdims=True)
        term = jnp.exp(score - top)
        part = nn(term.astype(BF), v * masks[n]) / jnp.sum(term, axis=1, keepdims=True)
        total = part if total is None else total + part
    out_ref[rows, :] = total.astype(BF)


MESH = pl.DeviceIdType.MESH


class Ring:
    def __init__(self, full, send, recv):
        h = lax.axis_index("head")
        y, c = h // 2, h % 2
        self.full, self.send, self.recv, self.used = full, send, recv, []
        self.own = h
        self.up = ((y + 1) % 4) * 2 + c
        self.dn = ((y + 3) % 4) * 2 + c
        self.op = ((y + 2) % 4) * 2 + c
        self.flip = 1 - 2 * c
        self.sib = h + self.flip

    def copy(self, block, start, size, to, sem, land):
        view = self.full.at[pl.ds(block * 128 + start, size), :]
        copy = pltpu.make_async_remote_copy(
            src_ref=view, dst_ref=view, send_sem=self.send.at[sem], recv_sem=self.recv.at[land],
            device_id={"head": to}, device_id_type=MESH,
        )
        copy.start()
        self.used.append(copy)
        return copy

    def begin(self):
        own = self.own
        self.dn_a = self.copy(own, 0, 64, self.up, 0, 0)
        self.up_b = self.copy(own, 64, 64, self.dn, 1, 3)
        self.side = self.copy(own, 0, 128, self.sib, 4, 6)
        self.dn_b = self.copy(own, 64, 64, self.up, 2, 1)
        self.up_a = self.copy(own, 0, 64, self.dn, 3, 2)

    def forward(self):
        self.dn_a.wait_recv()
        self.op_a = self.copy(self.dn, 0, 64, self.up, 5, 4)
        self.side_dn_a = self.copy(self.dn, 0, 64, self.sib, 6, 7)
        self.up_b.wait_recv()
        self.op_b = self.copy(self.up, 64, 64, self.dn, 7, 5)
        self.side_up_b = self.copy(self.up, 64, 64, self.sib, 8, 8)

    def near(self):
        self.dn_b.wait_recv()
        self.side_dn_b = self.copy(self.dn, 64, 64, self.sib, 9, 9)
        self.up_a.wait_recv()
        self.side_up_a = self.copy(self.up, 0, 64, self.sib, 10, 10)

    def far(self):
        self.op_a.wait_recv()
        self.side_op_a = self.copy(self.op, 0, 64, self.sib, 11, 11)
        self.op_b.wait_recv()
        self.side_op_b = self.copy(self.op, 64, 64, self.sib, 12, 12)

    def finish(self):
        for copy in self.used:
            copy.wait_send()


def head_sum():
    row = lax.broadcasted_iota(jnp.int32, (1024, 128), 0) // 64
    col = lax.broadcasted_iota(jnp.int32, (1024, 128), 1)
    return (row == col).astype(F32).astype(BF)


def head_spread():
    row = lax.broadcasted_iota(jnp.int32, (128, 1024), 0)
    col = lax.broadcasted_iota(jnp.int32, (128, 1024), 1) // 64
    return (row == col).astype(F32).astype(BF)


NX, NZ = 4, 8
A, B = slice(0, 64), slice(64, 128)


def middle(grid_ref, wf_ref, est_ref, kv, query, bg, mix):
    hsum = head_sum()
    spread = head_spread()

    def part(i, _):
        at = pl.multiple_of(i * 128, 128)
        rows = [pl.ds(at + e * 256, 128) for e in range(3)]
        qf = query[pl.ds(at, 128), :].astype(F32)
        back = bg[pl.ds(at, 128), :]
        products = [(qf * kv[r, :1024].astype(F32)).astype(BF) for r in rows]
        products += [(back * kv[r, 1024:].astype(F32)).astype(BF) for r in rows]
        sums = nn(jnp.concatenate(products, axis=0), hsum)
        score = [sums[e * 128 : e * 128 + 128] * SCALE for e in range(3)]
        along = [sums[e * 128 + 384 : e * 128 + 512] for e in range(3)]
        top = jnp.maximum(jnp.maximum(score[0], score[1]), score[2])
        term = [jnp.exp(s - top) for s in score]
        total = term[0] + term[1] + term[2]
        weight = [t / total for t in term]
        mean = weight[0] * along[0] + weight[1] * along[1] + weight[2] * along[2]
        heads = [w.astype(BF) for w in weight]
        heads += [(w * (s - mean) * SCALE).astype(BF) for w, s in zip(weight, along)]
        mixed = jnp.zeros((128, 1024), F32)
        for e in range(3):
            wide = nn(heads[e], spread)
            mixed += wide * kv[rows[e], 1024:].astype(F32)
            grad = nn(heads[3 + e], spread)
            kv[rows[e], :1024] = (grad * qf).astype(BF)
            kv[rows[e], 1024:] = (wide * back).astype(BF)
        mix[pl.ds(at, 128), :] = mixed.astype(BF)
        return 0

    lax.fori_loop(0, 2, part, 0)
    est_ref[...] = grid_ref[0:100, :].astype(F32) + nt(wf_ref[...], mix[...])


DMA = pltpu.SemaphoreType.DMA
SCRATCH = {
    "grid_v": ((112, 256), BF), "emb_v": ((128, 1024), BF), "src_v": ((16, 128), jnp.int32),
    "len_v": ((1, 128), jnp.int32), "wkv_v": ((112, 2048), BF), "pgain_v": ((1, 1024), F32),
    "wqkv_v": ((1024, 384), BF), "dgain_v": ((1, 1024), F32), "hid": ((128, 1024), F32),
    "full": ((1024, 1024), BF), "wfull": ((1024, 1024), BF), "q": ((1024, 128), BF),
    "kx": ((1536, 128), BF), "vx": ((1536, 128), BF), "att": ((1024, 128), BF), "afull": ((128, 1024), BF),
    "unit": ((128, 1024), F32), "inv": ((128, 128), F32), "send_v": ((32, 32), jnp.int32),
    "mine": ((NZ, 8, 128), jnp.int32), "dfc_v": ((100, 256), BF), "dsrc_v": ((3, 256), jnp.int32),
    "wq_v": ((112, 1024), BF), "wf_v": ((100, 1024), BF), "u_v": ((1024, 2048), BF),
    "zbuf": ((NZ, 128, 1024), BF), "tab": ((NZ, 8, 128), jnp.int32), "xs": ((8, 128, 1024), BF),
    "arrived": ((8, 128, 1024), BF), "kv": ((768, 2048), BF), "query": ((256, 1024), BF),
    "bg": ((256, 1024), F32), "mix": ((256, 1024), BF), "rg": ((768, 1024), BF),
    "bs": ((8, 128, 1024), BF), "rback": ((8, 128, 1024), BF), "outs": ((2, 4, 128, 1024), BF),
    "ins": ((2, 4, 128, 1024), BF),
}
SEMS = {
    "load": 18, "nsend": 13, "nrecv": 13, "wsend": 13, "wrecv": 13, "hsend": 4, "hrecv": 4, "asend": 8,
    "arecv": 8, "tsend": 8, "trecv": 8, "zsend": 16, "zrecv": 16, "xsend": 32, "xrecv": 32, "bsend": 32,
    "brecv": 32, "qsend": 16, "qrecv": 16,
}
INPUTS = (
    "grid_h", "emb_h", "src_h", "len_h", "wkv_h", "pgain_h", "wqkv_h", "wout_h", "dgain_h", "u_h", "wq_h",
    "wf_h", "send_h", "dsrc_h", "dfc_h",
)


class Refs:
    def __init__(self, refs):
        for name, ref in zip(INPUTS + ("est_o", "vert_o") + tuple(SCRATCH) + tuple(SEMS), refs):
            setattr(self, name, ref)


def start_loads(r, h):
    own = pl.ds(pl.multiple_of(h * 128, 128), 128)
    pairs = [
        (r.wout_h, r.wfull.at[own, :]), (r.send_h, r.send_v), (r.grid_h, r.grid_v), (r.emb_h, r.emb_v),
        (r.src_h, r.src_v), (r.len_h, r.len_v), (r.wkv_h, r.wkv_v), (r.pgain_h, r.pgain_v),
        (r.wqkv_h.at[0], r.wqkv_v.at[:, 0:128]), (r.wqkv_h.at[1], r.wqkv_v.at[:, 128:256]),
        (r.wqkv_h.at[2], r.wqkv_v.at[:, 256:384]), (r.dgain_h, r.dgain_v), (r.dfc_h, r.dfc_v),
        (r.dsrc_h, r.dsrc_v), (r.wq_h, r.wq_v), (r.wf_h, r.wf_v), (r.u_h, r.u_v),
    ]
    loads = [pltpu.make_async_copy(s, d, r.load.at[i]) for i, (s, d) in enumerate(pairs)]
    for copy in loads:
        copy.start()
    return loads


def kernel(*refs):
    r = Refs(refs)
    g = lax.axis_index("grp")
    h = lax.axis_index("head")
    groups = lax.axis_size("grp")
    right, left = (g + 1) % groups, (g + groups - 1) % groups
    x, z = g // NZ, g % NZ
    nexts = [(z + 1) % NZ, (z + NZ - 1) % NZ]
    loads = start_loads(r, h)
    barrier = pltpu.get_barrier_semaphore()
    for i in range(1, 8):
        pl.semaphore_signal(barrier, inc=1, device_id={"head": (h + i) % 8}, device_id_type=MESH)
    for k in range(1, NZ):
        pl.semaphore_signal(barrier, inc=1, device_id={"grp": x * NZ + (z + k) % NZ}, device_id_type=MESH)
    for k in range(1, NX):
        pl.semaphore_signal(barrier, inc=1, device_id={"grp": (x + k) % NX * NZ + z}, device_id_type=MESH)
    for other in (right, left):
        pl.semaphore_signal(barrier, inc=1, device_id={"grp": other}, device_id_type=MESH)
    loads[1].wait()
    table = jnp.concatenate([r.send_v[8 * k : 8 * k + 8, :] for k in range(NX)], axis=1)
    for k in range(NZ):
        r.mine[k] = jnp.broadcast_to(table[k : k + 1, :], (8, 128))
    pl.semaphore_wait(barrier, 7 + NZ + NX - 2 + 2)
    loads[0].wait()
    weights = Ring(r.wfull, r.wsend, r.wrecv)
    weights.begin()

    def remote(source, target, send, recv, xx, zz):
        copy = pltpu.make_async_remote_copy(
            src_ref=source, dst_ref=target, send_sem=send, recv_sem=recv,
            device_id={"grp": xx * NZ + zz}, device_id_type=MESH,
        )
        copy.start()
        return copy

    r.tab[pl.ds(z, 1)] = r.mine[pl.ds(z, 1)]
    tables = [
        remote(r.mine.at[(z + k) % NZ], r.tab.at[z], r.tsend.at[k], r.trecv.at[k], x, (z + k) % NZ)
        for k in range(1, NZ)
    ]
    for copy in loads[2:8]:
        copy.wait()
    encode(r.grid_v, r.emb_v, r.src_v, r.len_v, r.wkv_v, r.hid)
    unit, _ = norm_rows(r.hid[...])
    r.full[pl.ds(pl.multiple_of(h * 128, 128), 128), :] = (unit * r.pgain_v[...]).astype(BF)
    rows = Ring(r.full, r.nsend, r.nrecv)
    rows.begin()
    for copy in loads[8:16]:
        copy.wait()

    def project(block):
        at = pl.multiple_of(block * 128, 128)
        triple = nn(r.full[pl.ds(at, 128), :], r.wqkv_v[...]).astype(BF)
        r.q[pl.ds(at, 128), :] = (triple[:, :128].astype(F32) * SCALE).astype(BF)
        r.kx[pl.ds(at + 256, 128), :] = triple[:, 128:256]
        r.vx[pl.ds(at + 256, 128), :] = triple[:, 256:]

    flip = rows.flip
    project(h)
    rows.side.wait_recv()
    rows.forward()
    project(rows.sib)
    rows.near()
    project(rows.dn)
    project(rows.up)
    rows.side_dn_a.wait_recv()
    rows.side_dn_b.wait_recv()
    project(rows.dn + flip)
    rows.side_up_a.wait_recv()
    rows.side_up_b.wait_recv()
    project(rows.up + flip)
    rows.far()
    project(rows.op)
    rows.side_op_a.wait_recv()
    rows.side_op_b.wait_recv()
    project(rows.op + flip)

    halos = []
    for i, ref in enumerate((r.kx, r.vx)):
        for j, (start, land, to) in enumerate(((1024, 0, right), (256, 1280, left))):
            copy = pltpu.make_async_remote_copy(
                src_ref=ref.at[pl.ds(start, 256), :], dst_ref=ref.at[pl.ds(land, 256), :],
                send_sem=r.hsend.at[i * 2 + j], recv_sem=r.hrecv.at[i * 2 + j],
                device_id={"grp": to}, device_id_type=MESH,
            )
            copy.start()
            halos.append(copy)
    weights.forward()
    weights.near()

    def give(start, column, to, land):
        return pltpu.make_async_remote_copy(
            src_ref=r.att.at[pl.ds(start, 128), :], dst_ref=r.afull.at[:, pl.ds(column, 128)],
            send_sem=r.asend.at[to], recv_sem=r.arecv.at[land],
            device_id={"head": to}, device_id_type=MESH,
        )

    mine = pl.multiple_of(h * 128, 128)
    for blk in (1, 2, 0, 3):
        if blk == 0:
            weights.far()
            for copy in halos:
                copy.wait_recv()
        low = jnp.where(g == 0, 256, 0) if blk == 0 else 0
        high = jnp.where(g == groups - 1, 512, 768) if blk == 3 else 768
        attend(r.q, r.kx, r.vx, r.att, blk, low, high)
        for to in (2 * blk, 2 * blk + 1):

            @pl.when(to != h)
            def _():
                give(to * 128, mine, to, h).start()

    r.afull[:, pl.ds(mine, 128)] = r.att[pl.ds(mine, 128), :]
    r.query[...] = tn(r.grid_v[...], r.wq_v[...]).astype(BF)
    r.bg[...] = tn(r.dfc_v[...], r.wf_v[...])
    three = jnp.concatenate([r.dsrc_v[...], jnp.zeros((5, 256), jnp.int32)], axis=0)
    edges = three.astype(F32).T.astype(jnp.int32)
    for copy in (
        weights.side, weights.side_dn_a, weights.side_dn_b, weights.side_up_a, weights.side_up_b,
        weights.side_op_a, weights.side_op_b,
    ):
        copy.wait_recv()
    for other in range(8):

        @pl.when(other != h)
        def _():
            give(0, other * 128, other, other).wait()

    unit, inverse = norm_rows(r.hid[...] + nn(r.afull[...], r.wfull[...]))
    r.zbuf[z] = (unit * r.dgain_v[...]).astype(BF)
    sent = list(tables) + halos
    ring = {}

    def pass_on(way, d, chunk):
        block = (z + d) % NZ if way else (z + NZ - d) % NZ
        view = r.zbuf.at[block, pl.ds(64 * chunk, 64), :]
        sem = way * 8 + d * 2 + chunk
        ring[way, d, chunk] = remote(view, view, r.zsend.at[sem], r.zrecv.at[sem], x, nexts[way])
        sent.append(ring[way, d, chunk])

    hops = ((0, 0), (1, 1), (0, 1), (1, 0))
    for way, chunk in hops:
        pass_on(way, 0, chunk)
    r.unit[...] = unit
    r.inv[...] = jnp.broadcast_to(inverse, (128, 128))

    def where(index):
        if index == 0:
            return z
        return (z + (NZ - (index + 1) // 2 if index % 2 else index // 2)) % NZ

    def chosen(zz):
        node = lax.broadcasted_iota(jnp.int32, (128, 128), 0)
        return (node == r.tab[zz][0:1, :]).astype(F32).astype(BF)

    crossing = {}
    land = pl.ds(pl.multiple_of(x * 32, 32), 32)

    def select(index):
        zz = where(index)
        r.xs[index] = tn(chosen(zz), r.zbuf[zz]).astype(BF)
        for k in range(1, NX):
            xx = (x + k) % NX
            sem = index * NX + k
            crossing[index, k] = remote(
                r.xs.at[index, pl.ds(pl.multiple_of(xx * 32, 32), 32), :], r.arrived.at[index, land, :],
                r.xsend.at[sem], r.xrecv.at[sem], xx, z,
            )
        r.arrived[index, land, :] = r.xs[index, land, :]

    def absorb(first, count, tiles):
        if tiles[0] == 0:
            for index in range(first, first + count):
                for k in range(1, NX):
                    crossing[index, k].wait_recv()
        lane = lax.broadcasted_iota(jnp.int32, (1, 128), 1)
        slots = jnp.concatenate(
            [(lane // 32 * NZ + where(first + j)) * 32 + lane % 32 for j in range(count)], axis=1
        )
        picks = jnp.concatenate(
            [(edges[:, e : e + 1] == slots).astype(F32).astype(BF) for e in range(3)], axis=0
        )

        def tile(j, _):
            cols = pl.ds(pl.multiple_of(j * 256, 256), 256)
            block = r.arrived[first : first + count].reshape(count * 128, 1024)
            value = nn(picks, nn(block, r.u_v[:, cols]).astype(BF)).astype(BF)
            r.kv[:, cols] = value if first == 0 else r.kv[:, cols] + value
            return 0

        lax.fori_loop(*tiles, tile, 0)

    for copy in tables:
        copy.wait_recv()
    loads[16].wait()
    select(0)
    for d in range(1, 5):
        for way, chunk in hops:
            if d == 3 and (way, chunk) == (0, 1):
                absorb(0, 3, (4, 8))
            last = way == chunk
            if d < 4 or last:
                ring[way, d - 1, chunk].wait_recv()
            if d < 3 or (d == 3 and last):
                pass_on(way, d, chunk)
        if d < 4:
            select(2 * d - 1)
            select(2 * d)
        else:
            select(7)
        if d == 2:
            absorb(0, 3, (0, 4))
    absorb(3, 2, (0, 8))
    absorb(5, 2, (0, 8))
    absorb(7, 1, (0, 8))
    middle(r.grid_v, r.wf_v, r.est_o, r.kv, r.query, r.bg, r.mix)

    def unproject(j, _):
        cols = pl.ds(pl.multiple_of(j * 256, 256), 256)
        r.rg[:, cols] = nt(r.kv[...], r.u_v[cols, :]).astype(BF)
        return 0

    lax.fori_loop(0, 4, unproject, 0)
    returning = {}

    def scatter(index):
        zz = where(index)
        row = lax.broadcasted_iota(jnp.int32, (128, 256), 0)
        slot = (row // 32 * NZ + zz) * 32 + row % 32
        pick = jnp.concatenate(
            [(r.dsrc_v[e : e + 1, :] == slot).astype(F32).astype(BF) for e in range(3)], axis=1
        )
        r.bs[index] = nn(pick, r.rg[...]).astype(BF)
        for k in range(1, NX):
            xx = (x + k) % NX
            sem = index * NX + k
            returning[index, k] = remote(
                r.bs.at[index, pl.ds(pl.multiple_of(xx * 32, 32), 32), :], r.rback.at[index, land, :],
                r.bsend.at[sem], r.brecv.at[sem], xx, z,
            )
        r.rback[index, land, :] = r.bs[index, land, :]

    def partial(index):
        for k in range(1, NX):
            returning[index, k].wait_recv()
        return nn(chosen(where(index)), r.rback[index])

    flow = {}

    def push(way, i, chunk):
        rows = pl.ds(64 * chunk, 64)
        sem = way * 8 + i * 2 + chunk
        flow[way, i, chunk] = remote(
            r.outs.at[way, i, rows, :], r.ins.at[way, i, rows, :], r.qsend.at[sem], r.qrecv.at[sem],
            x, nexts[way],
        )

    def step(d):
        for way in range(2):
            part = partial(2 * d - way)
            for chunk in (way, 1 - way):
                rows = B if chunk else A
                value = part[rows]
                if d < 3 or chunk == way:
                    flow[way, d, chunk].wait_recv()
                    value = value + r.ins[way, d, rows].astype(F32)
                r.outs[way, d - 1, rows] = value.astype(BF)
                push(way, d - 1, chunk)

    scatter(7)
    scatter(6)
    scatter(5)
    part = partial(7)
    r.outs[0, 3, A] = part[A].astype(BF)
    push(0, 3, 0)
    r.outs[1, 3, B] = part[B].astype(BF)
    push(1, 3, 1)
    scatter(4)
    scatter(3)
    step(3)
    scatter(2)
    scatter(1)
    scatter(0)
    step(2)
    step(1)
    part = partial(0)
    for way in range(2):
        for chunk in range(2):
            flow[way, 0, chunk].wait_recv()
    grad = part + r.ins[0, 0].astype(F32) + r.ins[1, 0].astype(F32)
    unit = r.unit[...]
    scaled = grad * r.dgain_v[...]
    first = jnp.mean(scaled, axis=-1, keepdims=True)
    second = jnp.mean(scaled * unit, axis=-1, keepdims=True)
    r.vert_o[...] = r.inv[:, 0:1] * (scaled - first - unit * second)
    rows.finish()
    weights.finish()
    for copy in sent + list(crossing.values()) + list(returning.values()) + list(flow.values()):
        copy.wait_send()


VM = pl.BlockSpec(memory_space=pltpu.VMEM)
OUT = (jax.ShapeDtypeStruct((100, 256), F32), jax.ShapeDtypeStruct((128, 1024), F32))


def hand_over(a_ref, b_ref, c_ref, d_ref):
    c_ref[...] = a_ref[...]
    d_ref[...] = b_ref[...]


def body(
    grid_in, mesh_embed, enc_src, enc_len, enc_kv_weight, proc_gain, qkv_weight, out_weight,
    dec_gain, unpack, wq, wf, dec_send, dec_src, dforecast,
):
    est, vert = pl.pallas_call(
        kernel,
        out_shape=OUT,
        in_specs=[pl.BlockSpec(memory_space=pl.ANY)] * 15,
        out_specs=(VM, VM),
        scratch_shapes=[pltpu.VMEM(*s) for s in SCRATCH.values()] + [DMA((n,)) for n in SEMS.values()],
        compiler_params=pltpu.CompilerParams(
            vmem_limit_bytes=60 * 2**20, collective_id=0, has_side_effects=True
        ),
    )(
        grid_in, mesh_embed, enc_src, enc_len.reshape(1, -1), enc_kv_weight, proc_gain.reshape(1, -1),
        qkv_weight.transpose(1, 0, 2), out_weight, dec_gain.reshape(1, -1), unpack, wq, wf, dec_send,
        dec_src, dforecast,
    )
    return pl.pallas_call(
        hand_over, out_shape=OUT, in_specs=[VM, VM], out_specs=(VM, VM)
    )(est, vert)


def solution(mesh):
    return jax.shard_map(
        body,
        mesh=mesh,
        in_specs=(
            P(None, ("grp", "head")), P(("grp", "head"), None), P(None, ("grp", "head")),
            P(("grp", "head")), P(), P(), P(None, None, "head"), P("head", None), P(), P(), P(), P(),
            P(("grp", "head"), None), P(None, ("grp", "head")), P(None, ("grp", "head")),
        ),
        out_specs=(P(None, ("grp", "head")), P(("grp", "head"), None)),
        check_vma=False,
    )
```

time: 186 us -> 128 us (0.69)
  waiting for transfers between devices: 100 us -> 0 us
  Pallas kernels: 64 us -> 127 us
  starting transfers between devices: 11.6 us -> 0 us
  local copies, waits for them, and re-layouts: 4.93 us -> 0 us
  matrix products: 3.59 us -> 0 us
    all_to_all x2 -> x0, waiting for transfers between devices: 100 us -> none  [the longest x1 50.1 us: body(): lax.all_to_all(sent.reshape(32, 32, 1024), 'grp', 0, 0, tiled=True)]
    pallas_call x2, Pallas kernels: 64 us -> 127 us  [the longest x1 125 us: body(): pl.pallas_call(kernel, out_shape=OUT, in_specs=[pl.BlockSpec(memory_space...]
    all_to_all x2 -> x0, starting transfers between devices: 11.6 us -> none  [the longest x1 6.37 us: body(): lax.all_to_all(back.reshape(32, 32, 1024), 'grp', 0, 0, tiled=True)]
    dot_general x2 -> x0, matrix products: 3.59 us -> none  [the longest x1 3.05 us: body(): sent = jnp.dot(pick, dec_in, preferred_element_type=F32).astype(BF)]
    unnamed x20 -> x0, local copies, waits for them, and re-layouts: 2.87 us -> none
  transfers between devices with their start and end apart: 2 -> 0, of which waited for: 2 -> 0; matrix products, arithmetic and copies ran while one was open for 0% -> 0% of each run, Pallas kernels for 0% -> 0%
where the time goes in v4:
time: 128 us
  Pallas kernels  127 us (99%)
    pallas_call x1, Pallas kernels, body(): pl.pallas_call(kernel, out_shape=OUT, in_specs=[pl.BlockSpec(memory_space...  125 us

profile of v4, /device:TPU:24, one launch (start us, length us, event | category | flops | bytes accessed | tf_op | source)
XLA Modules:
  0.0 128.1 jit_solution(11745927836781498175)
XLA Ops:
  0.6 125.5 %shard_map.158 = (f32[100,256]{1,0:T(8,128)}, f32[128,1024]{1,0:T(8,128)}) custom-call(bf16[112,256]{1,0:T(8,128)(2,1)} %refs_0_.1, bf16[128,1024]{1,0:T(8,128)(2,1)} %refs_1_.1, s32[16,128]{1,0:T(8,128)} %refs_2_.1, s32[1,128]{1,0:T(1,128)} %bitcast.7, bf16[112,2048]{1,0:T(8,128)(2,1)} %refs_4_.1, f32[1,1024]{1,0:T(1,128)} %bitcast.5, ...), custom_call_target="tpu_custom_call" | custom-call | tf_op jit(solution)/shard_map/pallas_call | solution.py:564
  126.1 1.9 %shard_map.159 = (f32[100,256]{1,0:T(8,128)}, f32[128,1024]{1,0:T(8,128)}) custom-call(f32[100,256]{1,0:T(8,128)} %get-tuple-element.4.a_ref, f32[128,1024]{1,0:T(8,128)} %get-tuple-element.5.b_ref), custom_call_target="tpu_custom_call" | custom-call | tf_op jit(solution)/shard_map/pallas_call | solution.py:578

commit v5 on v4

--- a/solution.py
+++ b/solution.py
@@ -50,8 +50,8 @@
     masks = half_masks()
 
     def pair(j, _):
-        cols = pl.ds(pl.multiple_of(j * 128, 128), 128)
-        vcols = pl.ds(pl.multiple_of(j * 128 + 1024, 128), 128)
+        cols = pl.ds(j * 128, 128)
+        vcols = pl.ds(j * 128 + 1024, 128)
         keys = nn(grid_t, wkv_ref[:, cols]).astype(BF)
         values = nn(grid_t, wkv_ref[:, vcols]).astype(BF)
         emb = emb_ref[:, cols]
@@ -65,16 +65,17 @@
         hid_ref[:, cols] = emb.astype(F32) + mixed
         return 0
 
-    lax.fori_loop(0, emb_ref.shape[1] // 128, pair, 0)
-
-
-def attend(q_ref, k_ref, v_ref, out_ref, blk, low, high):
+    for j in range(emb_ref.shape[1] // 128):
+        pair(j, 0)
+
+
+def attend(q_ref, kv_ref, out_ref, blk, low, high):
     masks = half_masks()
     rows = pl.ds(blk * 256, 256)
     span = pl.ds(blk * 256, 768)
     q = q_ref[rows, :]
-    k = k_ref[span, :]
-    v = v_ref[span, :]
+    k = kv_ref[span, 0:128]
+    v = kv_ref[span, 128:256]
     gap = lax.broadcasted_iota(jnp.int32, (256, 768), 1) - lax.broadcasted_iota(
         jnp.int32, (256, 768), 0
     )
@@ -161,10 +162,10 @@
 
 
 NX, NZ = 4, 8
-A, B = slice(0, 64), slice(64, 128)
-
-
-def middle(grid_ref, wf_ref, est_ref, kv, query, bg, mix):
+HALF = (slice(0, 512), slice(512, 1024))
+
+
+def middle(kv, query, bg, mix):
     hsum = head_sum()
     spread = head_spread()
 
@@ -196,7 +197,6 @@
         return 0
 
     lax.fori_loop(0, 2, part, 0)
-    est_ref[...] = grid_ref[0:100, :].astype(F32) + nt(wf_ref[...], mix[...])
 
 
 DMA = pltpu.SemaphoreType.DMA
@@ -205,20 +205,20 @@
     "len_v": ((1, 128), jnp.int32), "wkv_v": ((112, 2048), BF), "pgain_v": ((1, 1024), F32),
     "wqkv_v": ((1024, 384), BF), "dgain_v": ((1, 1024), F32), "hid": ((128, 1024), F32),
     "full": ((1024, 1024), BF), "wfull": ((1024, 1024), BF), "q": ((1024, 128), BF),
-    "kx": ((1536, 128), BF), "vx": ((1536, 128), BF), "att": ((1024, 128), BF), "afull": ((128, 1024), BF),
+    "kvx": ((1536, 256), BF), "att": ((1024, 128), BF), "afull": ((128, 1024), BF),
     "unit": ((128, 1024), F32), "inv": ((128, 128), F32), "send_v": ((32, 32), jnp.int32),
     "mine": ((NZ, 8, 128), jnp.int32), "dfc_v": ((100, 256), BF), "dsrc_v": ((3, 256), jnp.int32),
     "wq_v": ((112, 1024), BF), "wf_v": ((100, 1024), BF), "u_v": ((1024, 2048), BF),
     "zbuf": ((NZ, 128, 1024), BF), "tab": ((NZ, 8, 128), jnp.int32), "xs": ((8, 128, 1024), BF),
-    "arrived": ((8, 128, 1024), BF), "kv": ((768, 2048), BF), "query": ((256, 1024), BF),
+    "arrived": ((8, 128, 1024), BF), "xe": ((768, 1024), BF), "kv": ((768, 2048), BF), "query": ((256, 1024), BF),
     "bg": ((256, 1024), F32), "mix": ((256, 1024), BF), "rg": ((768, 1024), BF),
     "bs": ((8, 128, 1024), BF), "rback": ((8, 128, 1024), BF), "outs": ((2, 4, 128, 1024), BF),
     "ins": ((2, 4, 128, 1024), BF),
 }
 SEMS = {
     "load": 18, "nsend": 13, "nrecv": 13, "wsend": 13, "wrecv": 13, "hsend": 4, "hrecv": 4, "asend": 8,
-    "arecv": 8, "tsend": 8, "trecv": 8, "zsend": 16, "zrecv": 16, "xsend": 32, "xrecv": 32, "bsend": 32,
-    "brecv": 32, "qsend": 16, "qrecv": 16,
+    "arecv": 8, "tsend": 8, "trecv": 8, "zsend": 16, "zrecv": 16, "xsend": 64, "xrecv": 64, "bsend": 64,
+    "brecv": 64, "qsend": 16, "qrecv": 16,
 }
 INPUTS = (
     "grid_h", "emb_h", "src_h", "len_h", "wkv_h", "pgain_h", "wqkv_h", "wout_h", "dgain_h", "u_h", "wq_h",
@@ -297,12 +297,26 @@
     for copy in loads[8:16]:
         copy.wait()
 
+    def halo(start, land, sem, to):
+        return pltpu.make_async_remote_copy(
+            src_ref=r.kvx.at[pl.ds(start, 128), :], dst_ref=r.kvx.at[pl.ds(land, 128), :],
+            send_sem=r.hsend.at[sem], recv_sem=r.hrecv.at[sem],
+            device_id={"grp": to}, device_id_type=MESH,
+        )
+
     def project(block):
         at = pl.multiple_of(block * 128, 128)
         triple = nn(r.full[pl.ds(at, 128), :], r.wqkv_v[...]).astype(BF)
         r.q[pl.ds(at, 128), :] = (triple[:, :128].astype(F32) * SCALE).astype(BF)
-        r.kx[pl.ds(at + 256, 128), :] = triple[:, 128:256]
-        r.vx[pl.ds(at + 256, 128), :] = triple[:, 256:]
+        r.kvx[pl.ds(at + 256, 128), :] = triple[:, 128:]
+
+        @pl.when(block >= 6)
+        def _():
+            halo(at + 256, at - 768, block - 6, right).start()
+
+        @pl.when(block < 2)
+        def _():
+            halo(at + 256, at + 1280, block + 2, left).start()
 
     flip = rows.flip
     project(h)
@@ -324,16 +338,9 @@
     rows.side_op_b.wait_recv()
     project(rows.op + flip)
 
-    halos = []
-    for i, ref in enumerate((r.kx, r.vx)):
-        for j, (start, land, to) in enumerate(((1024, 0, right), (256, 1280, left))):
-            copy = pltpu.make_async_remote_copy(
-                src_ref=ref.at[pl.ds(start, 256), :], dst_ref=ref.at[pl.ds(land, 256), :],
-                send_sem=r.hsend.at[i * 2 + j], recv_sem=r.hrecv.at[i * 2 + j],
-                device_id={"grp": to}, device_id_type=MESH,
-            )
-            copy.start()
-            halos.append(copy)
+    halos = [
+        halo(1024, 0, 0, right), halo(1152, 128, 1, right), halo(256, 1280, 2, left), halo(384, 1408, 3, left),
+    ]
     weights.forward()
     weights.near()
 
@@ -352,7 +359,7 @@
                 copy.wait_recv()
         low = jnp.where(g == 0, 256, 0) if blk == 0 else 0
         high = jnp.where(g == groups - 1, 512, 768) if blk == 3 else 768
-        attend(r.q, r.kx, r.vx, r.att, blk, low, high)
+        attend(r.q, r.kvx, r.att, blk, low, high)
         for to in (2 * blk, 2 * blk + 1):
 
             @pl.when(to != h)
@@ -382,7 +389,7 @@
 
     def pass_on(way, d, chunk):
         block = (z + d) % NZ if way else (z + NZ - d) % NZ
-        view = r.zbuf.at[block, pl.ds(64 * chunk, 64), :]
+        view = r.zbuf.at[block, :, pl.ds(512 * chunk, 512)]
         sem = way * 8 + d * 2 + chunk
         ring[way, d, chunk] = remote(view, view, r.zsend.at[sem], r.zrecv.at[sem], x, nexts[way])
         sent.append(ring[way, d, chunk])
@@ -405,23 +412,24 @@
     crossing = {}
     land = pl.ds(pl.multiple_of(x * 32, 32), 32)
 
-    def select(index):
+    def select(index, half):
         zz = where(index)
-        r.xs[index] = tn(chosen(zz), r.zbuf[zz]).astype(BF)
+        cols = pl.ds(512 * half, 512)
+        r.xs[index, :, HALF[half]] = tn(chosen(zz), r.zbuf[zz, :, HALF[half]]).astype(BF)
         for k in range(1, NX):
             xx = (x + k) % NX
-            sem = index * NX + k
-            crossing[index, k] = remote(
-                r.xs.at[index, pl.ds(pl.multiple_of(xx * 32, 32), 32), :], r.arrived.at[index, land, :],
+            sem = index * 8 + half * NX + k
+            crossing[index, half, k] = remote(
+                r.xs.at[index, pl.ds(pl.multiple_of(xx * 32, 32), 32), cols], r.arrived.at[index, land, cols],
                 r.xsend.at[sem], r.xrecv.at[sem], xx, z,
             )
-        r.arrived[index, land, :] = r.xs[index, land, :]
-
-    def absorb(first, count, tiles):
-        if tiles[0] == 0:
-            for index in range(first, first + count):
+        r.arrived[index, land, HALF[half]] = r.xs[index, land, HALF[half]]
+
+    def absorb(first, count):
+        for index in range(first, first + count):
+            for half in range(2):
                 for k in range(1, NX):
-                    crossing[index, k].wait_recv()
+                    crossing[index, half, k].wait_recv()
         lane = lax.broadcasted_iota(jnp.int32, (1, 128), 1)
         slots = jnp.concatenate(
             [(lane // 32 * NZ + where(first + j)) * 32 + lane % 32 for j in range(count)], axis=1
@@ -432,107 +440,110 @@
 
         def tile(j, _):
             cols = pl.ds(pl.multiple_of(j * 256, 256), 256)
-            block = r.arrived[first : first + count].reshape(count * 128, 1024)
-            value = nn(picks, nn(block, r.u_v[:, cols]).astype(BF)).astype(BF)
-            r.kv[:, cols] = value if first == 0 else r.kv[:, cols] + value
+            block = r.arrived[first : first + count, :, cols].reshape(count * 128, 256)
+            value = nn(picks, block).astype(BF)
+            r.xe[:, cols] = value if first == 0 else r.xe[:, cols] + value
             return 0
 
-        lax.fori_loop(*tiles, tile, 0)
+        lax.fori_loop(0, 4, tile, 0)
 
     for copy in tables:
         copy.wait_recv()
     loads[16].wait()
-    select(0)
+    select(0, 0)
+    select(0, 1)
     for d in range(1, 5):
-        for way, chunk in hops:
-            if d == 3 and (way, chunk) == (0, 1):
-                absorb(0, 3, (4, 8))
-            last = way == chunk
-            if d < 4 or last:
+        for phase in range(2):
+            if d == 4 and phase == 1:
+                continue
+            for way in range(2):
+                chunk = way ^ phase
                 ring[way, d - 1, chunk].wait_recv()
-            if d < 3 or (d == 3 and last):
-                pass_on(way, d, chunk)
-        if d < 4:
-            select(2 * d - 1)
-            select(2 * d)
-        else:
-            select(7)
-        if d == 2:
-            absorb(0, 3, (0, 4))
-    absorb(3, 2, (0, 8))
-    absorb(5, 2, (0, 8))
-    absorb(7, 1, (0, 8))
-    middle(r.grid_v, r.wf_v, r.est_o, r.kv, r.query, r.bg, r.mix)
+                if d < 3 or (d == 3 and phase == 0):
+                    pass_on(way, d, chunk)
+            for way in range(2):
+                select(7 if d == 4 else 2 * d - 1 + way, way ^ phase)
+            if d == 2 and phase == 1:
+                absorb(0, 3)
+        if d == 3:
+            absorb(3, 2)
+    absorb(5, 3)
+
+    def unpack(j, _):
+        cols = pl.ds(pl.multiple_of(j * 256, 256), 256)
+        r.kv[:, cols] = nn(r.xe[...], r.u_v[:, cols]).astype(BF)
+        return 0
+
+    lax.fori_loop(0, 8, unpack, 0)
+    middle(r.kv, r.query, r.bg, r.mix)
 
     def unproject(j, _):
         cols = pl.ds(pl.multiple_of(j * 256, 256), 256)
         r.rg[:, cols] = nt(r.kv[...], r.u_v[cols, :]).astype(BF)
         return 0
 
-    lax.fori_loop(0, 4, unproject, 0)
     returning = {}
 
-    def scatter(index):
-        zz = where(index)
-        row = lax.broadcasted_iota(jnp.int32, (128, 256), 0)
-        slot = (row // 32 * NZ + zz) * 32 + row % 32
-        pick = jnp.concatenate(
-            [(r.dsrc_v[e : e + 1, :] == slot).astype(F32).astype(BF) for e in range(3)], axis=1
-        )
-        r.bs[index] = nn(pick, r.rg[...]).astype(BF)
+    def scatter(half, *indices):
+        for index in indices:
+            zz = where(index)
+            row = lax.broadcasted_iota(jnp.int32, (128, 256), 0)
+            slot = (row // 32 * NZ + zz) * 32 + row % 32
+            pick = jnp.concatenate(
+                [(r.dsrc_v[e : e + 1, :] == slot).astype(F32).astype(BF) for e in range(3)], axis=1
+            )
+            r.bs[index, :, HALF[half]] = nn(pick, r.rg[:, HALF[half]]).astype(BF)
+            cols = pl.ds(512 * half, 512)
+            for k in range(1, NX):
+                xx = (x + k) % NX
+                sem = index * 8 + half * NX + k
+                returning[index, half, k] = remote(
+                    r.bs.at[index, pl.ds(pl.multiple_of(xx * 32, 32), 32), cols],
+                    r.rback.at[index, land, cols], r.bsend.at[sem], r.brecv.at[sem], xx, z,
+                )
+            r.rback[index, land, HALF[half]] = r.bs[index, land, HALF[half]]
+
+    def partial(index, half):
         for k in range(1, NX):
-            xx = (x + k) % NX
-            sem = index * NX + k
-            returning[index, k] = remote(
-                r.bs.at[index, pl.ds(pl.multiple_of(xx * 32, 32), 32), :], r.rback.at[index, land, :],
-                r.bsend.at[sem], r.brecv.at[sem], xx, z,
-            )
-        r.rback[index, land, :] = r.bs[index, land, :]
-
-    def partial(index):
-        for k in range(1, NX):
-            returning[index, k].wait_recv()
-        return nn(chosen(where(index)), r.rback[index])
+            returning[index, half, k].wait_recv()
+        return nn(chosen(where(index)), r.rback[index, :, HALF[half]])
 
     flow = {}
 
-    def push(way, i, chunk):
-        rows = pl.ds(64 * chunk, 64)
+    def push(way, i, chunk, value):
+        r.outs[way, i, :, HALF[chunk]] = value.astype(BF)
+        cols = pl.ds(512 * chunk, 512)
         sem = way * 8 + i * 2 + chunk
         flow[way, i, chunk] = remote(
-            r.outs.at[way, i, rows, :], r.ins.at[way, i, rows, :], r.qsend.at[sem], r.qrecv.at[sem],
+            r.outs.at[way, i, :, cols], r.ins.at[way, i, :, cols], r.qsend.at[sem], r.qrecv.at[sem],
             x, nexts[way],
         )
 
     def step(d):
-        for way in range(2):
-            part = partial(2 * d - way)
-            for chunk in (way, 1 - way):
-                rows = B if chunk else A
-                value = part[rows]
-                if d < 3 or chunk == way:
+        for phase in range(2):
+            for way in range(2):
+                chunk = way ^ phase
+                value = partial(2 * d - way, chunk)
+                if d < 3 or phase == 0:
                     flow[way, d, chunk].wait_recv()
-                    value = value + r.ins[way, d, rows].astype(F32)
-                r.outs[way, d - 1, rows] = value.astype(BF)
-                push(way, d - 1, chunk)
-
-    scatter(7)
-    scatter(6)
-    scatter(5)
-    part = partial(7)
-    r.outs[0, 3, A] = part[A].astype(BF)
-    push(0, 3, 0)
-    r.outs[1, 3, B] = part[B].astype(BF)
-    push(1, 3, 1)
-    scatter(4)
-    scatter(3)
+                    value = value + r.ins[way, d, :, HALF[chunk]].astype(F32)
+                push(way, d - 1, chunk, value)
+
+    lax.fori_loop(0, 2, unproject, 0)
+    scatter(0, 7, 6, 5)
+    lax.fori_loop(2, 4, unproject, 0)
+    scatter(1, 7, 6, 5)
+    push(0, 3, 0, partial(7, 0))
+    push(1, 3, 1, partial(7, 1))
+    scatter(0, 4, 3)
+    scatter(1, 4, 3)
+    r.est_o[...] = r.grid_v[0:100, :].astype(F32) + nt(r.wf_v[...], r.mix[...])
     step(3)
-    scatter(2)
-    scatter(1)
-    scatter(0)
+    scatter(0, 2, 1, 0)
+    scatter(1, 2, 1, 0)
     step(2)
     step(1)
-    part = partial(0)
+    part = jnp.concatenate([partial(0, 0), partial(0, 1)], axis=1)
     for way in range(2):
         for chunk in range(2):
             flow[way, 0, chunk].wait_recv()

time: 128 us -> 119 us (0.930)
  Pallas kernels: 127 us -> 118 us
    pallas_call x1, Pallas kernels: 125 us -> 116 us  [body(): pl.pallas_call(kernel, out_shape=OUT, in_specs=[pl.BlockSpec(memory_space...]
where the time goes in v5:
time: 119 us
  Pallas kernels  118 us (99%)
    pallas_call x1, Pallas kernels, body(): pl.pallas_call(kernel, out_shape=OUT, in_specs=[pl.BlockSpec(memory_space...  116 us

profile of v5, /device:TPU:24, one launch (start us, length us, event | category | flops | bytes accessed | tf_op | source)
XLA Modules:
  0.0 118.8 jit_solution(16180563805667747599)
XLA Ops:
  0.6 116.2 %shard_map.158 = (f32[100,256]{1,0:T(8,128)}, f32[128,1024]{1,0:T(8,128)}) custom-call(bf16[112,256]{1,0:T(8,128)(2,1)} %refs_0_.1, bf16[128,1024]{1,0:T(8,128)(2,1)} %refs_1_.1, s32[16,128]{1,0:T(8,128)} %refs_2_.1, s32[1,128]{1,0:T(1,128)} %bitcast.7, bf16[112,2048]{1,0:T(8,128)(2,1)} %refs_4_.1, f32[1,1024]{1,0:T(1,128)} %bitcast.5, ...), custom_call_target="tpu_custom_call" | custom-call | tf_op jit(solution)/shard_map/pallas_call | solution.py:575
  116.9 1.9 %shard_map.159 = (f32[100,256]{1,0:T(8,128)}, f32[128,1024]{1,0:T(8,128)}) custom-call(f32[100,256]{1,0:T(8,128)} %get-tuple-element.4.a_ref, f32[128,1024]{1,0:T(8,128)} %get-tuple-element.5.b_ref), custom_call_target="tpu_custom_call" | custom-call | tf_op jit(solution)/shard_map/pallas_call | solution.py:589

commit v6 on v5

--- a/solution.py
+++ b/solution.py
@@ -269,10 +269,6 @@
     table = jnp.concatenate([r.send_v[8 * k : 8 * k + 8, :] for k in range(NX)], axis=1)
     for k in range(NZ):
         r.mine[k] = jnp.broadcast_to(table[k : k + 1, :], (8, 128))
-    pl.semaphore_wait(barrier, 7 + NZ + NX - 2 + 2)
-    loads[0].wait()
-    weights = Ring(r.wfull, r.wsend, r.wrecv)
-    weights.begin()
 
     def remote(source, target, send, recv, xx, zz):
         copy = pltpu.make_async_remote_copy(
@@ -282,18 +278,21 @@
         copy.start()
         return copy
 
+    for copy in loads[2:8]:
+        copy.wait()
+    encode(r.grid_v, r.emb_v, r.src_v, r.len_v, r.wkv_v, r.hid)
+    unit, _ = norm_rows(r.hid[...])
+    r.full[pl.ds(pl.multiple_of(h * 128, 128), 128), :] = (unit * r.pgain_v[...]).astype(BF)
+    pl.semaphore_wait(barrier, 7 + NZ + NX - 2 + 2)
+    rows = Ring(r.full, r.nsend, r.nrecv)
+    rows.begin()
     r.tab[pl.ds(z, 1)] = r.mine[pl.ds(z, 1)]
     tables = [
         remote(r.mine.at[(z + k) % NZ], r.tab.at[z], r.tsend.at[k], r.trecv.at[k], x, (z + k) % NZ)
         for k in range(1, NZ)
     ]
-    for copy in loads[2:8]:
-        copy.wait()
-    encode(r.grid_v, r.emb_v, r.src_v, r.len_v, r.wkv_v, r.hid)
-    unit, _ = norm_rows(r.hid[...])
-    r.full[pl.ds(pl.multiple_of(h * 128, 128), 128), :] = (unit * r.pgain_v[...]).astype(BF)
-    rows = Ring(r.full, r.nsend, r.nrecv)
-    rows.begin()
+    loads[0].wait()
+    weights = Ring(r.wfull, r.wsend, r.wrecv)
     for copy in loads[8:16]:
         copy.wait()
 
@@ -324,6 +323,7 @@
     rows.forward()
     project(rows.sib)
     rows.near()
+    weights.begin()
     project(rows.dn)
     project(rows.up)
     rows.side_dn_a.wait_recv()
@@ -519,30 +519,42 @@
             x, nexts[way],
         )
 
-    def step(d):
-        for phase in range(2):
-            for way in range(2):
-                chunk = way ^ phase
-                value = partial(2 * d - way, chunk)
-                if d < 3 or phase == 0:
-                    flow[way, d, chunk].wait_recv()
-                    value = value + r.ins[way, d, :, HALF[chunk]].astype(F32)
-                push(way, d - 1, chunk, value)
+    def step(d, phase):
+        for way in range(2):
+            chunk = way ^ phase
+            value = partial(2 * d - way, chunk)
+            if d < 3 or phase == 0:
+                flow[way, d, chunk].wait_recv()
+                value = value + r.ins[way, d, :, HALF[chunk]].astype(F32)
+            push(way, d - 1, chunk, value)
 
     lax.fori_loop(0, 2, unproject, 0)
-    scatter(0, 7, 6, 5)
+    scatter(0, 7)
     lax.fori_loop(2, 4, unproject, 0)
-    scatter(1, 7, 6, 5)
+    scatter(1, 7)
+    scatter(1, 6)
+    scatter(0, 5)
     push(0, 3, 0, partial(7, 0))
     push(1, 3, 1, partial(7, 1))
-    scatter(0, 4, 3)
-    scatter(1, 4, 3)
+    scatter(0, 6)
+    scatter(1, 5)
+    scatter(1, 4)
+    step(3, 1)
+    scatter(0, 3)
+    scatter(0, 4)
+    scatter(1, 3)
     r.est_o[...] = r.grid_v[0:100, :].astype(F32) + nt(r.wf_v[...], r.mix[...])
-    step(3)
-    scatter(0, 2, 1, 0)
-    scatter(1, 2, 1, 0)
-    step(2)
-    step(1)
+    step(3, 0)
+    scatter(1, 2)
+    scatter(0, 1)
+    scatter(0, 2)
+    scatter(1, 1)
+    step(2, 1)
+    scatter(0, 0)
+    scatter(1, 0)
+    step(2, 0)
+    step(1, 1)
+    step(1, 0)
     part = jnp.concatenate([partial(0, 0), partial(0, 1)], axis=1)
     for way in range(2):
         for chunk in range(2):

time: 119 us -> 113 us (0.950)
  Pallas kernels: 118 us -> 112 us
    pallas_call x1, Pallas kernels: 116 us -> 110 us  [body(): pl.pallas_call(kernel, out_shape=OUT, in_specs=[pl.BlockSpec(memory_space...]
where the time goes in v6:
time: 113 us
  Pallas kernels  112 us (99%)
    pallas_call x1, Pallas kernels, body(): pl.pallas_call(kernel, out_shape=OUT, in_specs=[pl.BlockSpec(memory_space...  110 us

profile of v6, /device:TPU:24, one launch (start us, length us, event | category | flops | bytes accessed | tf_op | source)
XLA Modules:
  0.0 112.8 jit_solution(12714743002205523187)
XLA Ops:
  0.6 110.2 %shard_map.158 = (f32[100,256]{1,0:T(8,128)}, f32[128,1024]{1,0:T(8,128)}) custom-call(bf16[112,256]{1,0:T(8,128)(2,1)} %refs_0_.1, bf16[128,1024]{1,0:T(8,128)(2,1)} %refs_1_.1, s32[16,128]{1,0:T(8,128)} %refs_2_.1, s32[1,128]{1,0:T(1,128)} %bitcast.7, bf16[112,2048]{1,0:T(8,128)(2,1)} %refs_4_.1, f32[1,1024]{1,0:T(1,128)} %bitcast.5, ...), custom_call_target="tpu_custom_call" | custom-call | tf_op jit(solution)/shard_map/pallas_call | solution.py:587
  110.8 1.9 %shard_map.159 = (f32[100,256]{1,0:T(8,128)}, f32[128,1024]{1,0:T(8,128)}) custom-call(f32[100,256]{1,0:T(8,128)} %get-tuple-element.4.a_ref, f32[128,1024]{1,0:T(8,128)} %get-tuple-element.5.b_ref), custom_call_target="tpu_custom_call" | custom-call | tf_op jit(solution)/shard_map/pallas_call | solution.py:601

commit v7 on v6

--- a/solution.py
+++ b/solution.py
@@ -342,7 +342,6 @@
         halo(1024, 0, 0, right), halo(1152, 128, 1, right), halo(256, 1280, 2, left), halo(384, 1408, 3, left),
     ]
     weights.forward()
-    weights.near()
 
     def give(start, column, to, land):
         return pltpu.make_async_remote_copy(
@@ -354,7 +353,7 @@
     mine = pl.multiple_of(h * 128, 128)
     for blk in (1, 2, 0, 3):
         if blk == 0:
-            weights.far()
+            weights.near()
             for copy in halos:
                 copy.wait_recv()
         low = jnp.where(g == 0, 256, 0) if blk == 0 else 0
@@ -366,6 +365,7 @@
             def _():
                 give(to * 128, mine, to, h).start()
 
+    weights.far()
     r.afull[:, pl.ds(mine, 128)] = r.att[pl.ds(mine, 128), :]
     r.query[...] = tn(r.grid_v[...], r.wq_v[...]).astype(BF)
     r.bg[...] = tn(r.dfc_v[...], r.wf_v[...])
@@ -467,18 +467,19 @@
                 absorb(0, 3)
         if d == 3:
             absorb(3, 2)
-    absorb(5, 3)
+    absorb(5, 2)
+    absorb(7, 1)
 
     def unpack(j, _):
-        cols = pl.ds(pl.multiple_of(j * 256, 256), 256)
+        cols = pl.ds(pl.multiple_of(j * 1024, 1024), 1024)
         r.kv[:, cols] = nn(r.xe[...], r.u_v[:, cols]).astype(BF)
         return 0
 
-    lax.fori_loop(0, 8, unpack, 0)
+    lax.fori_loop(0, 2, unpack, 0)
     middle(r.kv, r.query, r.bg, r.mix)
 
     def unproject(j, _):
-        cols = pl.ds(pl.multiple_of(j * 256, 256), 256)
+        cols = pl.ds(pl.multiple_of(j * 512, 512), 512)
         r.rg[:, cols] = nt(r.kv[...], r.u_v[cols, :]).astype(BF)
         return 0
 
@@ -528,9 +529,9 @@
                 value = value + r.ins[way, d, :, HALF[chunk]].astype(F32)
             push(way, d - 1, chunk, value)
 
-    lax.fori_loop(0, 2, unproject, 0)
+    lax.fori_loop(0, 1, unproject, 0)
     scatter(0, 7)
-    lax.fori_loop(2, 4, unproject, 0)
+    lax.fori_loop(1, 2, unproject, 0)
     scatter(1, 7)
     scatter(1, 6)
     scatter(0, 5)

time: 113 us -> 109 us (0.965)
  Pallas kernels: 112 us -> 108 us
    pallas_call x1, Pallas kernels: 110 us -> 106 us  [body(): pl.pallas_call(kernel, out_shape=OUT, in_specs=[pl.BlockSpec(memory_space...]
where the time goes in v7:
time: 109 us
  Pallas kernels  108 us (99%)
    pallas_call x1, Pallas kernels, body(): pl.pallas_call(kernel, out_shape=OUT, in_specs=[pl.BlockSpec(memory_space...  106 us

profile of v7, /device:TPU:24, one launch (start us, length us, event | category | flops | bytes accessed | tf_op | source)
XLA Modules:
  0.0 108.5 jit_solution(17206631556653713832)
XLA Ops:
  0.6 105.9 %shard_map.158 = (f32[100,256]{1,0:T(8,128)}, f32[128,1024]{1,0:T(8,128)}) custom-call(bf16[112,256]{1,0:T(8,128)(2,1)} %refs_0_.1, bf16[128,1024]{1,0:T(8,128)(2,1)} %refs_1_.1, s32[16,128]{1,0:T(8,128)} %refs_2_.1, s32[1,128]{1,0:T(1,128)} %bitcast.7, bf16[112,2048]{1,0:T(8,128)(2,1)} %refs_4_.1, f32[1,1024]{1,0:T(1,128)} %bitcast.5, ...), custom_call_target="tpu_custom_call" | custom-call | tf_op jit(solution)/shard_map/pallas_call | solution.py:588
  106.6 1.9 %shard_map.159 = (f32[100,256]{1,0:T(8,128)}, f32[128,1024]{1,0:T(8,128)}) custom-call(f32[100,256]{1,0:T(8,128)} %get-tuple-element.4.a_ref, f32[128,1024]{1,0:T(8,128)} %get-tuple-element.5.b_ref), custom_call_target="tpu_custom_call" | custom-call | tf_op jit(solution)/shard_map/pallas_call | solution.py:602

commit v8 on v7

--- a/solution.py
+++ b/solution.py
@@ -218,7 +218,7 @@
 SEMS = {
     "load": 18, "nsend": 13, "nrecv": 13, "wsend": 13, "wrecv": 13, "hsend": 4, "hrecv": 4, "asend": 8,
     "arecv": 8, "tsend": 8, "trecv": 8, "zsend": 16, "zrecv": 16, "xsend": 64, "xrecv": 64, "bsend": 64,
-    "brecv": 64, "qsend": 16, "qrecv": 16,
+    "brecv": 64, "qsend": 32, "qrecv": 32,
 }
 INPUTS = (
     "grid_h", "emb_h", "src_h", "len_h", "wkv_h", "pgain_h", "wqkv_h", "wout_h", "dgain_h", "u_h", "wq_h",
@@ -511,23 +511,24 @@
 
     flow = {}
 
-    def push(way, i, chunk, value):
-        r.outs[way, i, :, HALF[chunk]] = value.astype(BF)
-        cols = pl.ds(512 * chunk, 512)
-        sem = way * 8 + i * 2 + chunk
-        flow[way, i, chunk] = remote(
-            r.outs.at[way, i, :, cols], r.ins.at[way, i, :, cols], r.qsend.at[sem], r.qrecv.at[sem],
-            x, nexts[way],
-        )
+    def push(way, i, chunk, value, wait):
+        for sub in range(2):
+            cols = pl.ds(512 * chunk + 256 * sub, 256)
+            part = value[:, 256 * sub : 256 * sub + 256]
+            if wait:
+                flow[way, i + 1, chunk, sub].wait_recv()
+                part = part + r.ins[way, i + 1, :, cols].astype(F32)
+            r.outs[way, i, :, cols] = part.astype(BF)
+            sem = way * 16 + i * 4 + chunk * 2 + sub
+            flow[way, i, chunk, sub] = remote(
+                r.outs.at[way, i, :, cols], r.ins.at[way, i, :, cols], r.qsend.at[sem], r.qrecv.at[sem],
+                x, nexts[way],
+            )
 
     def step(d, phase):
         for way in range(2):
             chunk = way ^ phase
-            value = partial(2 * d - way, chunk)
-            if d < 3 or phase == 0:
-                flow[way, d, chunk].wait_recv()
-                value = value + r.ins[way, d, :, HALF[chunk]].astype(F32)
-            push(way, d - 1, chunk, value)
+            push(way, d - 1, chunk, partial(2 * d - way, chunk), d < 3 or phase == 0)
 
     lax.fori_loop(0, 1, unproject, 0)
     scatter(0, 7)
@@ -535,8 +536,8 @@
     scatter(1, 7)
     scatter(1, 6)
     scatter(0, 5)
-    push(0, 3, 0, partial(7, 0))
-    push(1, 3, 1, partial(7, 1))
+    push(0, 3, 0, partial(7, 0), False)
+    push(1, 3, 1, partial(7, 1), False)
     scatter(0, 6)
     scatter(1, 5)
     scatter(1, 4)
@@ -558,8 +559,8 @@
     step(1, 0)
     part = jnp.concatenate([partial(0, 0), partial(0, 1)], axis=1)
     for way in range(2):
-        for chunk in range(2):
-            flow[way, 0, chunk].wait_recv()
+        for chunk in range(4):
+            flow[way, 0, chunk // 2, chunk % 2].wait_recv()
     grad = part + r.ins[0, 0].astype(F32) + r.ins[1, 0].astype(F32)
     unit = r.unit[...]
     scaled = grad * r.dgain_v[...]

time: 109 us -> 109 us (level)
  no operation moved by 1% of the time
where the time goes in v8:
time: 109 us
  Pallas kernels  108 us (99%)
    pallas_call x1, Pallas kernels, body(): pl.pallas_call(kernel, out_shape=OUT, in_specs=[pl.BlockSpec(memory_space...  106 us

profile of v8, /device:TPU:24, one launch (start us, length us, event | category | flops | bytes accessed | tf_op | source)
XLA Modules:
  0.0 108.7 jit_solution(17377650054906355365)
XLA Ops:
  0.6 106.1 %shard_map.158 = (f32[100,256]{1,0:T(8,128)}, f32[128,1024]{1,0:T(8,128)}) custom-call(bf16[112,256]{1,0:T(8,128)(2,1)} %refs_0_.1, bf16[128,1024]{1,0:T(8,128)(2,1)} %refs_1_.1, s32[16,128]{1,0:T(8,128)} %refs_2_.1, s32[1,128]{1,0:T(1,128)} %bitcast.7, bf16[112,2048]{1,0:T(8,128)(2,1)} %refs_4_.1, f32[1,1024]{1,0:T(1,128)} %bitcast.5, ...), custom_call_target="tpu_custom_call" | custom-call | tf_op jit(solution)/shard_map/pallas_call | solution.py:589
  106.7 1.9 %shard_map.159 = (f32[100,256]{1,0:T(8,128)}, f32[128,1024]{1,0:T(8,128)}) custom-call(f32[100,256]{1,0:T(8,128)} %get-tuple-element.4.a_ref, f32[128,1024]{1,0:T(8,128)} %get-tuple-element.5.b_ref), custom_call_target="tpu_custom_call" | custom-call | tf_op jit(solution)/shard_map/pallas_call | solution.py:603

commit v9 on v8

--- a/solution.py
+++ b/solution.py
@@ -242,7 +242,7 @@
         (r.dsrc_h, r.dsrc_v), (r.wq_h, r.wq_v), (r.wf_h, r.wf_v), (r.u_h, r.u_v),
     ]
     loads = [pltpu.make_async_copy(s, d, r.load.at[i]) for i, (s, d) in enumerate(pairs)]
-    for copy in loads:
+    for copy in loads[1:8]:
         copy.start()
     return loads
 
@@ -280,6 +280,8 @@
 
     for copy in loads[2:8]:
         copy.wait()
+    for copy in loads[8:] + loads[:1]:
+        copy.start()
     encode(r.grid_v, r.emb_v, r.src_v, r.len_v, r.wkv_v, r.hid)
     unit, _ = norm_rows(r.hid[...])
     r.full[pl.ds(pl.multiple_of(h * 128, 128), 128), :] = (unit * r.pgain_v[...]).astype(BF)
@@ -397,8 +399,6 @@
     hops = ((0, 0), (1, 1), (0, 1), (1, 0))
     for way, chunk in hops:
         pass_on(way, 0, chunk)
-    r.unit[...] = unit
-    r.inv[...] = jnp.broadcast_to(inverse, (128, 128))
 
     def where(index):
         if index == 0:
@@ -416,7 +416,7 @@
         zz = where(index)
         cols = pl.ds(512 * half, 512)
         r.xs[index, :, HALF[half]] = tn(chosen(zz), r.zbuf[zz, :, HALF[half]]).astype(BF)
-        for k in range(1, NX):
+        for k in (2, 1, 3):
             xx = (x + k) % NX
             sem = index * 8 + half * NX + k
             crossing[index, half, k] = remote(
@@ -452,6 +452,8 @@
     loads[16].wait()
     select(0, 0)
     select(0, 1)
+    r.unit[...] = unit
+    r.inv[...] = jnp.broadcast_to(inverse, (128, 128))
     for d in range(1, 5):
         for phase in range(2):
             if d == 4 and phase == 1:
@@ -495,7 +497,7 @@
             )
             r.bs[index, :, HALF[half]] = nn(pick, r.rg[:, HALF[half]]).astype(BF)
             cols = pl.ds(512 * half, 512)
-            for k in range(1, NX):
+            for k in (2, 1, 3):
                 xx = (x + k) % NX
                 sem = index * 8 + half * NX + k
                 returning[index, half, k] = remote(

time: 109 us -> 108 us (level)
  no operation moved by 1% of the time
where the time goes in v9:
time: 108 us
  Pallas kernels  107 us (99%)
    pallas_call x1, Pallas kernels, body(): pl.pallas_call(kernel, out_shape=OUT, in_specs=[pl.BlockSpec(memory_space...  106 us

profile of v9, /device:TPU:24, one launch (start us, length us, event | category | flops | bytes accessed | tf_op | source)
XLA Modules:
  0.0 108.1 jit_solution(12563372018220068115)
XLA Ops:
  0.6 105.5 %shard_map.158 = (f32[100,256]{1,0:T(8,128)}, f32[128,1024]{1,0:T(8,128)}) custom-call(bf16[112,256]{1,0:T(8,128)(2,1)} %refs_0_.1, bf16[128,1024]{1,0:T(8,128)(2,1)} %refs_1_.1, s32[16,128]{1,0:T(8,128)} %refs_2_.1, s32[1,128]{1,0:T(1,128)} %bitcast.7, bf16[112,2048]{1,0:T(8,128)(2,1)} %refs_4_.1, f32[1,1024]{1,0:T(1,128)} %bitcast.5, ...), custom_call_target="tpu_custom_call" | custom-call | tf_op jit(solution)/shard_map/pallas_call | solution.py:591
  106.2 1.9 %shard_map.159 = (f32[100,256]{1,0:T(8,128)}, f32[128,1024]{1,0:T(8,128)}) custom-call(f32[100,256]{1,0:T(8,128)} %get-tuple-element.4.a_ref, f32[128,1024]{1,0:T(8,128)} %get-tuple-element.5.b_ref), custom_call_target="tpu_custom_call" | custom-call | tf_op jit(solution)/shard_map/pallas_call | solution.py:605

commit v10 on v9

--- a/solution.py
+++ b/solution.py
@@ -76,14 +76,21 @@
     q = q_ref[rows, :]
     k = kv_ref[span, 0:128]
     v = kv_ref[span, 128:256]
-    gap = lax.broadcasted_iota(jnp.int32, (256, 768), 1) - lax.broadcasted_iota(
-        jnp.int32, (256, 768), 0
+    gap = lax.broadcasted_iota(jnp.int32, (256, 256), 1) - lax.broadcasted_iota(
+        jnp.int32, (256, 256), 0
     )
-    col = lax.broadcasted_iota(jnp.int32, (256, 768), 1)
-    live = (gap >= 0) & (gap <= 512) & (col >= low) & (col < high)
+    early, late = gap >= low, gap <= high
     total = None
     for n in range(2):
-        score = jnp.where(live, nt(q * masks[n], k), -jnp.inf)
+        score = nt(q * masks[n], k)
+        score = jnp.concatenate(
+            [
+                jnp.where(early, score[:, :256], -jnp.inf),
+                score[:, 256:512],
+                jnp.where(late, score[:, 512:], -jnp.inf),
+            ],
+            axis=1,
+        )
         top = jnp.max(score, axis=1, keepdims=True)
         term = jnp.exp(score - top)
         part = nn(term.astype(BF), v * masks[n]) / jnp.sum(term, axis=1, keepdims=True)
@@ -359,7 +366,7 @@
             for copy in halos:
                 copy.wait_recv()
         low = jnp.where(g == 0, 256, 0) if blk == 0 else 0
-        high = jnp.where(g == groups - 1, 512, 768) if blk == 3 else 768
+        high = jnp.where(g == groups - 1, -256, 0) if blk == 3 else 0
         attend(r.q, r.kvx, r.att, blk, low, high)
         for to in (2 * blk, 2 * blk + 1):
 

time: 108 us -> 108 us (level)
  no operation moved by 1% of the time
where the time goes in v10:
time: 108 us
  Pallas kernels  107 us (99%)
    pallas_call x1, Pallas kernels, body(): pl.pallas_call(kernel, out_shape=OUT, in_specs=[pl.BlockSpec(memory_space...  106 us

profile of v10, /device:TPU:24, one launch (start us, length us, event | category | flops | bytes accessed | tf_op | source)
XLA Modules:
  0.0 108.1 jit_solution(15399801038586682143)
XLA Ops:
  0.6 105.5 %shard_map.158 = (f32[100,256]{1,0:T(8,128)}, f32[128,1024]{1,0:T(8,128)}) custom-call(bf16[112,256]{1,0:T(8,128)(2,1)} %refs_0_.1, bf16[128,1024]{1,0:T(8,128)(2,1)} %refs_1_.1, s32[16,128]{1,0:T(8,128)} %refs_2_.1, s32[1,128]{1,0:T(1,128)} %bitcast.7, bf16[112,2048]{1,0:T(8,128)(2,1)} %refs_4_.1, f32[1,1024]{1,0:T(1,128)} %bitcast.5, ...), custom_call_target="tpu_custom_call" | custom-call | tf_op jit(solution)/shard_map/pallas_call | solution.py:598
  106.2 1.9 %shard_map.159 = (f32[100,256]{1,0:T(8,128)}, f32[128,1024]{1,0:T(8,128)}) custom-call(f32[100,256]{1,0:T(8,128)} %get-tuple-element.4.a_ref, f32[128,1024]{1,0:T(8,128)} %get-tuple-element.5.b_ref), custom_call_target="tpu_custom_call" | custom-call | tf_op jit(solution)/shard_map/pallas_call | solution.py:612
